TPU v7x, 32 devices: a whole 2x2x4 slice. The times are simulated.
32 devices in a mesh: cls: 4 (over x, core), dom: 8 (over z, y).
Axes of the slice: x: 2, y: 2, z: 4, core: 2. Of those that a mesh axis runs over, the one named last changes fastest.
Arguments:
- particles: bfloat16 [128, 36864], P(('cls', 'dom')), may hold values from -6 to 6
- references: bfloat16 [200, 36864], P('cls'), may hold values from -0.03125 to 0.03125
- candidates: int32 [128, 8], P(('cls', 'dom')), may hold values from 0 to 199, as said below
- offsets: int32 [128, 2], P(('cls', 'dom')), may hold values from -7 to 7
Outputs:
- class_average: bfloat16 [200, 36864], P('cls')
Inputs may be any that keep to these rules, and one draw needn't show every extreme that they name: `candidates`: each particle lists 8 distinct classes, 4 of them with each of two class owners, the owner of class c being c // (200 / number of cls groups). Of the 4 particles of one device at most 2 list classes of one owner, and on every device some owner is listed by exactly 2.
All inputs are finite; a program needn't handle non-finite values.
Results may differ from a plain program's by a relative error of at most 0.0074.
Values may be sent and summed in bfloat16 or wider, within the bound.
No kernel may reach another device: no remote copies, remote signals or barrier semaphores. Data moves between devices by JAX's collectives and lax.ppermute only.
A program may use at most 128 MiB of HBM per device.

v0:
```python
import math

import jax
import jax.numpy as jnp
from jax import lax
from jax.sharding import PartitionSpec as P

CYCLES = 128
ANGLES = 144
ROT = 36
SHIFTS = 5
BOX = 256


SOFTMAX_WARMTH = 2.0
PRIOR_MASS = 1.0
NEGATIVE = -1e30
SHIFT_X_STEPS = (0, 1, -1, 0, 0)
SHIFT_Y_STEPS = (0, 0, 0, 1, -1)


def phase_angles(move_x, move_y):
    theta = 2.0 * math.pi * jnp.arange(ANGLES, dtype=jnp.float32) / ANGLES
    radius = jnp.arange(1, CYCLES + 1, dtype=jnp.float32)
    along = (
        jnp.cos(theta)[:, None] * move_x.astype(jnp.float32)[..., None, None]
        + jnp.sin(theta)[:, None] * move_y.astype(jnp.float32)[..., None, None]
    )
    return 2.0 * math.pi / BOX * along * radius


def shift_images(images, phase):
    real_part = images[..., 0, :].astype(jnp.float32)
    imag_part = images[..., 1, :].astype(jnp.float32)
    cosine = jnp.cos(phase)
    sine = jnp.sin(phase)
    return jnp.stack(
        [real_part * cosine + imag_part * sine, imag_part * cosine - real_part * sine], axis=-2
    ).astype(jnp.bfloat16)


def shards(particles, references, candidates, offsets):
    groups = lax.axis_size("cls")
    owner = lax.axis_index("cls")
    count = particles.shape[0]
    capacity = count // 2
    local = references.shape[0]
    width = references.shape[1]
    listed_count = candidates.shape[1]
    block_width = width // ROT
    row_count = groups * capacity
    listed_owner = candidates // local
    group_index = jnp.arange(groups, dtype=jnp.int32)
    present = jnp.any(listed_owner[:, :, None] == group_index[None, None, :], axis=1)
    ranking = jnp.cumsum(present.astype(jnp.int32), axis=0) - 1
    slot_index = jnp.arange(capacity, dtype=jnp.int32)
    class_assignment = present.T[:, None, :] & (ranking.T[:, None, :] == slot_index[None, :, None])
    outgoing = jnp.einsum(
        "evd,do->evo",
        class_assignment.astype(jnp.bfloat16),
        particles,
        preferred_element_type=jnp.float32,
    ).astype(jnp.bfloat16)
    particle_index = jnp.arange(count, dtype=jnp.int32)
    particle_records = jnp.concatenate(
        [
            candidates.astype(jnp.float32),
            offsets.astype(jnp.float32),
            particle_index[:, None].astype(jnp.float32),
            jnp.ones((count, 1), jnp.float32),
            jnp.zeros((count, 4), jnp.float32),
        ],
        axis=1,
    )
    meta_out = jnp.einsum(
        "yhu,um->yhm",
        class_assignment.astype(jnp.float32),
        particle_records,
        precision=lax.Precision.HIGHEST,
    ).astype(jnp.bfloat16)
    arrived, arrived_meta = (
        lax.all_to_all(outgoing, "cls", split_axis=0, concat_axis=0, tiled=True),
        lax.all_to_all(meta_out, "cls", split_axis=0, concat_axis=0, tiled=True),
    )
    details = arrived_meta.astype(jnp.float32).reshape(row_count, -1)
    listed = details[:, :listed_count].astype(jnp.int32)
    prior_x = details[:, listed_count].astype(jnp.int32)
    prior_y = details[:, listed_count + 1].astype(jnp.int32)
    filled = details[:, listed_count + 3] > 0.5
    class_index = owner * local + jnp.arange(local, dtype=jnp.int32)
    allowed = jnp.any(listed[:, :, None] == class_index[None, None, :], axis=1) & filled[:, None]
    turn_index = jnp.arange(ROT, dtype=jnp.int32)
    diagonal = (
        turn_index[None, :, None] == (turn_index[:, None, None] - turn_index[None, None, :]) % ROT
    )
    diagonal_f32 = diagonal.astype(jnp.float32)
    diagonal_bf16 = diagonal.astype(jnp.bfloat16)
    class_refs = references.reshape(local, ROT, block_width)
    images = arrived.reshape(row_count, ANGLES, 2, CYCLES)
    moved_list = []
    score_list = []
    for shift in range(SHIFTS):
        phase = phase_angles(prior_x + SHIFT_X_STEPS[shift], prior_y + SHIFT_Y_STEPS[shift])
        moved = shift_images(images, phase).reshape(row_count, ROT, block_width)
        pairs = jnp.einsum("xjf,clf->xjcl", moved, class_refs, preferred_element_type=jnp.float32)
        score_values = SOFTMAX_WARMTH * jnp.einsum(
            "xjcl,jlr->xcr", pairs, diagonal_f32, precision=lax.Precision.HIGHEST
        )
        moved_list.append(moved)
        score_list.append(score_values)
    all_scores = jnp.stack(score_list, axis=1)
    allowed_wide = allowed[:, None, :, None]
    local_max = jnp.max(jnp.where(allowed_wide, all_scores, NEGATIVE), axis=(1, 2, 3))
    local_sum = jnp.sum(
        jnp.exp(jnp.where(allowed_wide, all_scores - local_max[:, None, None, None], NEGATIVE)),
        axis=(1, 2, 3),
    )
    back_max, back_sum = (
        lax.all_to_all(
            local_max.reshape(groups, capacity), "cls", split_axis=0, concat_axis=0, tiled=True
        ),
        lax.all_to_all(
            local_sum.reshape(groups, capacity), "cls", split_axis=0, concat_axis=0, tiled=True
        ),
    )
    owner_max = jnp.max(jnp.where(class_assignment, back_max[:, :, None], NEGATIVE), axis=1)
    owner_sum = jnp.sum(jnp.where(class_assignment, back_sum[:, :, None], 0.0), axis=1)
    whole_max = jnp.max(owner_max, axis=0)
    whole_sum = jnp.sum(owner_sum * jnp.exp(owner_max - whole_max[None, :]), axis=0)
    slot_max = jnp.sum(jnp.where(class_assignment, whole_max[None, None, :], 0.0), axis=2)
    slot_sum = jnp.sum(jnp.where(class_assignment, whole_sum[None, None, :], 0.0), axis=2)
    total_max, total_sum = (
        lax.all_to_all(slot_max, "cls", split_axis=0, concat_axis=0, tiled=True),
        lax.all_to_all(slot_sum, "cls", split_axis=0, concat_axis=0, tiled=True),
    )
    total_max = total_max.reshape(row_count)
    total_sum = total_sum.reshape(row_count)
    safe_sum = jnp.where(filled, total_sum, 1.0)
    totals = jnp.zeros((local, ROT, block_width), jnp.float32)
    masses = jnp.zeros((local,), jnp.float32)
    for shift in range(SHIFTS):
        exponent = jnp.exp(
            jnp.where(allowed[:, :, None], score_list[shift] - total_max[:, None, None], NEGATIVE)
        )
        weight = (exponent / safe_sum[:, None, None]).astype(jnp.bfloat16)
        masses = masses + jnp.sum(weight.astype(jnp.float32), axis=(0, 2))
        spread = jnp.einsum(
            "xcr,jlr->xcjl", weight, diagonal_bf16, preferred_element_type=jnp.float32
        ).astype(jnp.bfloat16)
        totals = totals + jnp.einsum(
            "xcjl,xjf->clf", spread, moved_list[shift], preferred_element_type=jnp.float32
        )
    totals = totals.reshape(local, width)
    piece = lax.psum_scatter(totals, "dom", scatter_dimension=1, tiled=True)
    summed_mass = lax.psum(masses, "dom")
    average_piece = (piece / (summed_mass + PRIOR_MASS)[:, None]).astype(jnp.bfloat16)
    return lax.all_gather(average_piece, "dom", axis=1, tiled=True)


def solution(mesh):
    in_specs = (
        P(("cls", "dom"), None),
        P("cls", None),
        P(("cls", "dom"), None),
        P(("cls", "dom"), None),
    )
    out_specs = P("cls", None)
    return jax.shard_map(shards, mesh=mesh, in_specs=in_specs, out_specs=out_specs, check_vma=False)
```

profile of v0, /device:TPU:0, one launch (start us, length us, event | category | flops | bytes accessed | tf_op | source)
XLA Modules:
  0.0 496.5 jit_solution(9664861918433876321)
XLA Ops:
  9.4 4.2 all-to-all-start
  15.5 7.1 %reshape.599 = bf16[50,36,1024]{2,1,0:T(8,128)(2,1)} reshape(bf16[50,36864]{1,0:T(8,128)(2,1)} %param.5) | data formatting | bytes 7372800 | tf_op jit(solution)/shard_map/reshape | solution.py:98
  23.1 3.7 all-to-all-start.1
  27.5 8.8 %all-to-all-done.1 = bf16[4,2,36864]{2,1,0:T(2,128)(2,1)S(1)} async-done(((bf16[4,2,36864]{2,1,0:T(2,128)(2,1)}), bf16[4,2,36864]{2,1,0:T(2,128)(2,1)S(1)}, u32[]{:S(2)}, u32[]{:S(2)}) %all-to-all-start.1) | async-done | bytes 589856 | tf_op jit(solution)/shard_map/all_to_all | solution.py:82
  40.2 11.6 %fusion.41 = (bf16[8,144,1,128]{3,1,2,0:T(8,128)(2,1)S(1)}, bf16[8,144,1,128]{3,1,2,0:T(8,128)(2,1)S(1)}, bf16[8,144,1,128]{3,1,2,0:T(8,128)(2,1)S(1)}, bf16[8,1...) fusion(bf16[8,144,1,128]{3,1,2,0:T(8,128)(2,1)S(1)} %get-tuple-, ...), kind=kLoop, calls=%fused_computation.96 | loop fusion | flops 6340608 | bytes 3267584 | tf_op jit(solution)/shard_map/add | solution.py:38
  55.3 11.2 %fusion.4 = f32[8,36,50,36]{2,1,3,0:T(8,128)} fusion(bf16[50,36,1024]{2,1,0:T(8,128)(2,1)} %reshape.599, bf16[8,36,1024,1]{2,1,0,3:T(8,128)(2,1)} %reshape.614), kind=kOutput, calls=%fused_computation.9 | convolution fusion | flops 1061683200 | bytes 6349824 | tf_op jit(solution)/shard_map/xjf,clf->xjcl/dot_general | solution.py:105
  66.5 8.7 %fusion.6 = f32[8,36,50,36]{2,1,3,0:T(8,128)} fusion(bf16[50,36,1024]{2,1,0:T(8,128)(2,1)S(1)} %copy-done.2, bf16[8,36,1024,1]{2,1,0,3:T(8,128)(2,1)S(1)} %copy-done.6), kind=kOutput, calls=%fused_computation.11 | convolution fusion | flops 1061683200 | bytes 6349824 | tf_op jit(solution)/shard_map/xjf,clf->xjcl/dot_general | solution.py:105
  76.2 11.3 %fusion.8 = f32[8,36,50,36]{2,1,3,0:T(8,128)} fusion(bf16[50,36,1024]{2,1,0:T(8,128)(2,1)} %reshape.599, bf16[8,36,1024,1]{2,1,0,3:T(8,128)(2,1)S(1)} %reshape.606), kind=kOutput, calls=%fused_computation.13 | convolution fusion | flops 1061683200 | bytes 6349824 | tf_op jit(solution)/shard_map/xjf,clf->xjcl/dot_general | solution.py:105
  88.3 11.6 %fusion.2 = f32[8,36,50,36]{2,1,3,0:T(8,128)} fusion(bf16[50,36,1024]{2,1,0:T(8,128)(2,1)} %reshape.599, bf16[8,36,1024,1]{2,1,0,3:T(8,128)(2,1)S(1)} %reshape.618), kind=kOutput, calls=%fused_computation.7 | convolution fusion | flops 1061683200 | bytes 6349824 | tf_op jit(solution)/shard_map/xjf,clf->xjcl/dot_general | solution.py:105
  100.9 6.7 %fusion = f32[8,36,50,36]{2,1,3,0:T(8,128)S(1)} fusion(bf16[50,36,1024]{2,1,0:T(8,128)(2,1)} %reshape.599, bf16[8,36,1024,1]{2,1,0,3:T(8,128)(2,1)S(1)} %reshape.622), kind=kOutput, calls=%fused_computation.5 | convolution fusion | flops 1061683200 | bytes 6349824 | tf_op jit(solution)/shard_map/xjf,clf->xjcl/dot_general | solution.py:105
  107.6 5.5 %bitcast_dynamic-update-slice_fusion.4 = (f32[8,5,50,36]{2,3,0,1:T(8,128)S(1)}, f32[8,50,36]{1,2,0:T(8,128)S(1)}) fusion(f32[8,36,50,36]{2,1,3,0:T(8,128)} %fusion.8, pred[36,36,36]{0,2,1:T(8,128)(4,1)S(1)} %copy.82), kind=kOutput, calls=%fused_computation.110 | convolution fusion | flops 223963200 | bytes 2447936 | tf_op jit(solution)/shard_map/xjcl,jlr->xcr/dot_general | solution.py:106
  113.2 5.5 %bitcast_dynamic-update-slice_fusion.3 = (f32[8,5,50,36]{2,3,0,1:T(8,128)S(1)}, f32[8,50,36]{1,2,0:T(8,128)S(1)}) fusion(f32[8,5,50,36]{2,3,0,1:T(8,128)S(1)} %get-tuple-element.62, f32[8,36,50,36]{2,1,3,0:T(8,128)} %fusion.6, pred[36,36,36]{0,2,1:T(8,128)(4,1)S(1)} %copy.82), kind=kOutput, calls=%fused_computation.109 | convolution fusion | flops 223963200 | bytes 2585600 | tf_op jit(solution)/shard_map/xjcl,jlr->xcr/dot_general | solution.py:106
  128.4 6.1 %all_to_all.46 = f32[4,1,2]{2,1,0:T(1,128)S(1)} all-to-all(f32[4,1,2]{2,1,0:T(1,128)S(1)} %bitcast.191), channel_id=1, replica_groups=mesh['cls'=4,'dom'=8] {'cls'}, dimensions={0} | all-to-all | bytes 64 | tf_op jit(solution)/shard_map/all_to_all | solution.py:122
  134.5 3.2 all-to-all-start.2
  137.8 3.5 all-to-all-done.2
  142.3 3.2 all-to-all-start.5
  149.2 3.2 all-to-all-start.3
  158.0 9.1 %copy.102 = bf16[8,50,36,36]{2,3,0,1:T(8,128)(2,1)} copy(bf16[8,50,36,36]{1,3,2,0:T(8,128)(2,1)S(1)} %convolution_convert_fusion.4) | data formatting | bytes 2073600 | tf_op jit(solution)/shard_map/convert_element_type | solution.py:149
  167.0 8.0 %fusion.74 = f32[50,36,1024,1]{2,1,3,0:T(8,128)} fusion(bf16[8,50,36,36]{2,3,0,1:T(8,128)(2,1)} %copy.102, bf16[8,36,1024,1]{2,1,0,3:T(8,128)(2,1)} %reshape.610), kind=kOutput, calls=%fused_computation.180 | convolution fusion | flops 1061683200 | bytes 8999424 | tf_op jit(solution)/shard_map/xcjl,xjf->clf/dot_general | solution.py:150
  175.9 8.8 %copy.103 = bf16[8,50,36,36]{2,3,0,1:T(8,128)(2,1)} copy(bf16[8,50,36,36]{1,3,2,0:T(8,128)(2,1)S(1)} %convolution_convert_fusion.3) | data formatting | bytes 2073600 | tf_op jit(solution)/shard_map/convert_element_type | solution.py:149
  184.8 8.0 %fusion.75 = f32[50,36,1024,1]{2,1,3,0:T(8,128)} fusion(bf16[8,50,36,36]{2,3,0,1:T(8,128)(2,1)} %copy.103, bf16[8,36,1024,1]{2,1,0,3:T(8,128)(2,1)} %reshape.614), kind=kOutput, calls=%fused_computation.181 | convolution fusion | flops 1061683200 | bytes 8999424 | tf_op jit(solution)/shard_map/xcjl,xjf->clf/dot_general | solution.py:150
  193.7 9.1 %copy.101 = bf16[8,50,36,36]{2,3,0,1:T(8,128)(2,1)} copy(bf16[8,50,36,36]{1,3,2,0:T(8,128)(2,1)S(1)} %convolution_convert_fusion.5) | data formatting | bytes 2073600 | tf_op jit(solution)/shard_map/convert_element_type | solution.py:149
  202.8 8.1 %fusion.73 = f32[50,36,1024,1]{2,1,3,0:T(8,128)} fusion(bf16[8,50,36,36]{2,3,0,1:T(8,128)(2,1)} %copy.101, bf16[8,36,1024,1]{2,1,0,3:T(8,128)(2,1)} %copy-done.4), kind=kOutput, calls=%fused_computation.179 | convolution fusion | flops 1061683200 | bytes 8999424 | tf_op jit(solution)/shard_map/xcjl,xjf->clf/dot_general | solution.py:150
  211.8 8.8 %copy.104 = bf16[8,50,36,36]{2,3,0,1:T(8,128)(2,1)} copy(bf16[8,50,36,36]{1,3,2,0:T(8,128)(2,1)S(1)} %convolution_convert_fusion.2) | data formatting | bytes 2073600 | tf_op jit(solution)/shard_map/convert_element_type | solution.py:149
  220.6 8.1 %fusion.76 = f32[50,36,1024,1]{2,1,3,0:T(8,128)} fusion(bf16[8,50,36,36]{2,3,0,1:T(8,128)(2,1)} %copy.104, bf16[8,36,1024,1]{2,1,0,3:T(8,128)(2,1)} %copy-done.5), kind=kOutput, calls=%fused_computation.182 | convolution fusion | flops 1061683200 | bytes 8999424 | tf_op jit(solution)/shard_map/xcjl,xjf->clf/dot_general | solution.py:150
  229.6 9.1 %copy.105 = bf16[8,50,36,36]{2,3,0,1:T(8,128)(2,1)} copy(bf16[8,50,36,36]{1,3,2,0:T(8,128)(2,1)S(1)} %convolution_convert_fusion.1) | data formatting | bytes 2073600 | tf_op jit(solution)/shard_map/convert_element_type | solution.py:149
  238.7 15.4 %bitcast_add_fusion = f32[50,36,1024]{2,1,0:T(8,128)S(1)} fusion(f32[50,36,1024,1]{2,1,3,0:T(8,128)} %fusion.76, f32[50,36,1024,1]{2,1,3,0:T(8,128)} %fusion.75, f32[50,36,1024,1]{2,1,3,0:T(8,128)} %fusion.74, f32[50,36,1024,1]{2,1,3,0:T(8,128)} %fusion.73, bf16[8,50,36,36]{2,3,0,1:T(8,128)(2,1)} %copy.105, bf16[8,36,1024,1]{2,1,0,3:T(8,128)(2,1)} %copy-done.3), kind=kOutput, calls=%fused_computation.1 | convolution fusion | flops 1069056000 | bytes 38490624 | tf_op jit(solution)/shard_map/xcjl,xjf->clf/dot_general | solution.py:150
  255.2 7.8 %copy.128 = f32[7,8,36,1024]{3,1,2,0:T(8,128)} copy(f32[7,8,36,1024]{3,2,1,0:T(8,128)S(1)} %bitcast.184) | data formatting | bytes 16515072
  263.1 22.4 %psum.7 = f32[50]{0:T(128)S(1)} all-reduce(f32[50]{0:T(128)S(1)} %add_add_fusion), channel_id=1, replica_groups=mesh['cls'=4,'dom'=8] {'dom'}, use_global_device_ids=true, to_apply=%region_17.18 | all-reduce | flops 50 | bytes 400 | tf_op jit(solution)/shard_map/psum | solution.py:155
  285.5 125.4 %reduce-scatter.2.cloned.1.call-done = f32[50,4608]{1,0:T(8,128)} async-done(((f32[50,36864]{1,0:T(8,128)}), f32[50,4608]{1,0:T(8,128)}) %reduce-scatter.2.cloned.1.call-update) | async-done | bytes 921616 | tf_op jit(solution)/shard_map/reduce_scatter | solution.py:154
  413.0 71.7 %all-gather.2.cloned.1.call-done = bf16[50,36864]{1,0:T(8,128)(2,1)} async-done(((bf16[50,4608]{1,0:T(8,128)(2,1)}), bf16[50,36864]{1,0:T(8,128)(2,1)}) %all-gather.2.cloned.1.call-update) | async-done | bytes 3686416 | tf_op jit(solution)/shard_map/all_gather | solution.py:157
  484.8 4.4 copy.156
  (110 shorter events, 42.5 us)
Async XLA Ops:
  6.5 7.1 %copy-start = (bf16[4,36864]{1,0:T(4,128)(2,1)S(1)}, bf16[4,36864]{1,0:T(4,128)(2,1)}, u32[]{:S(2)}) copy-start(bf16[4,36864]{1,0:T(4,128)(2,1)} %param.4) | copy-start | bytes 884740
  9.4 13.8 %all-to-all-start = ((bf16[4,2,16]{2,1,0:T(2,128)(2,1)}), bf16[4,2,16]{2,1,0:T(2,128)(2,1)S(1)}, u32[]{:S(2)}, u32[]{:S(2)}) async-start(bf16[4,2,16]{2,1,0:T(2,128)(2,1)} %copy.76), calls=%async_computation | async-start | bytes 4096 | tf_op jit(solution)/shard_map/all_to_all | solution.py:83
  23.1 13.2 %all-to-all-start.1 = ((bf16[4,2,36864]{2,1,0:T(2,128)(2,1)}), bf16[4,2,36864]{2,1,0:T(2,128)(2,1)S(1)}, u32[]{:S(2)}, u32[]{:S(2)}) async-start(bf16[4,2,36864]{2,1,0:T(2,128)(2,1)} %copy.77), calls=%async_computation.1 | async-start | bytes 1179648 | tf_op jit(solution)/shard_map/all_to_all | solution.py:82
  55.3 11.3 %copy-start.2 = (bf16[50,36,1024]{2,1,0:T(8,128)(2,1)S(1)}, bf16[50,36,1024]{2,1,0:T(8,128)(2,1)}, u32[]{:S(2)}) copy-start(bf16[50,36,1024]{2,1,0:T(8,128)(2,1)} %reshape.599) | copy-start | bytes 11059204
  55.3 11.3 %copy-start.6 = (bf16[8,36,1024,1]{2,1,0,3:T(8,128)(2,1)S(1)}, bf16[8,36,1024,1]{2,1,0,3:T(8,128)(2,1)}, u32[]{:S(2)}) copy-start(bf16[8,36,1024,1]{2,1,0,3:T(8,128)(2,1)} %reshape.610) | copy-start | bytes 1769476
  76.1 11.3 %copy-start.4 = (bf16[8,36,1024,1]{2,1,0,3:T(8,128)(2,1)}, bf16[8,36,1024,1]{2,1,0,3:T(8,128)(2,1)S(1)}, u32[]{:S(2)}) copy-start(bf16[8,36,1024,1]{2,1,0,3:T(8,128)(2,1)S(1)} %reshape.606) | copy-start | bytes 1769476
  88.3 11.7 %copy-start.5 = (bf16[8,36,1024,1]{2,1,0,3:T(8,128)(2,1)}, bf16[8,36,1024,1]{2,1,0,3:T(8,128)(2,1)S(1)}, u32[]{:S(2)}) copy-start(bf16[8,36,1024,1]{2,1,0,3:T(8,128)(2,1)S(1)} %reshape.618) | copy-start | bytes 1769476
  100.0 18.6 %slice-start = ((s8[5898240]{0:T(1024)(128)(4,1)}), s8[1703936]{0:T(1024)(128)(4,1)S(1)}, s32[]{:S(2)}) async-start(s8[5898240]{0:T(1024)(128)(4,1)} %bitcast.186), calls=%async_computation.9 | async-start | bytes 3407872
  100.8 6.8 %copy-start.3 = (bf16[8,36,1024,1]{2,1,0,3:T(8,128)(2,1)}, bf16[8,36,1024,1]{2,1,0,3:T(8,128)(2,1)S(1)}, u32[]{:S(2)}) copy-start(bf16[8,36,1024,1]{2,1,0,3:T(8,128)(2,1)S(1)} %reshape.622) | copy-start | bytes 1769476
  100.9 17.8 %slice-start.1 = ((s8[5898240]{0:T(1024)(128)(4,1)}), s8[4194304]{0:T(1024)(128)(4,1)S(1)}, s32[]{:S(2)}) async-start(s8[5898240]{0:T(1024)(128)(4,1)} %bitcast.186), calls=%async_computation.10 | async-start | bytes 8388608
  107.6 13.9 %slice-start.2 = ((s8[5898240]{0:T(1024)(128)(4,1)}), s8[4194304]{0:T(1024)(128)(4,1)S(1)}, s32[]{:S(2)}) async-start(s8[5898240]{0:T(1024)(128)(4,1)} %bitcast.188), calls=%async_computation.11 | async-start | bytes 8388608
  113.1 8.4 %slice-start.3 = ((s8[5898240]{0:T(1024)(128)(4,1)}), s8[1703936]{0:T(1024)(128)(4,1)S(1)}, s32[]{:S(2)}) async-start(s8[5898240]{0:T(1024)(128)(4,1)} %bitcast.188), calls=%async_computation.12 | async-start | bytes 3407872
  134.5 6.9 %all-to-all-start.2 = ((f32[4,1,2]{2,1,0:T(1,128)}), f32[4,1,2]{2,1,0:T(1,128)S(1)}, u32[]{:S(2)}, u32[]{:S(2)}) async-start(f32[4,1,2]{2,1,0:T(1,128)} %bitcast.36), calls=%async_computation.2 | async-start | bytes 4096 | tf_op jit(solution)/shard_map/all_to_all | solution.py:119
  142.3 6.9 %all-to-all-start.5 = ((f32[4,1,2]{2,1,0:T(1,128)}), f32[4,1,2]{2,1,0:T(1,128)S(1)}, u32[]{:S(2)}, u32[]{:S(2)}) async-start(f32[4,1,2]{2,1,0:T(1,128)} %copy.100), calls=%async_computation.5 | async-start | bytes 4096 | tf_op jit(solution)/shard_map/all_to_all | solution.py:134
  149.2 6.8 %all-to-all-start.3 = ((f32[4,1,2]{2,1,0:T(1,128)}), f32[4,1,2]{2,1,0:T(1,128)S(1)}, u32[]{:S(2)}, u32[]{:S(2)}) async-start(f32[4,1,2]{2,1,0:T(1,128)} %copy.97), calls=%async_computation.3 | async-start | bytes 4096 | tf_op jit(solution)/shard_map/all_to_all | solution.py:133
  152.4 258.4 %reduce-scatter.2.cloned.1.call-start = ((), (), s32[]{:S(2)}) async-start(), calls=%async_computation.7 | async-start | bytes 9289728 | tf_op jit(solution)/shard_map/reduce_scatter | solution.py:154
  263.0 221.8 %all-gather.2.cloned.1.call-start = ((), (), s32[]{:S(2)}) async-start(), calls=%async_computation.8 | async-start | bytes 4644864 | tf_op jit(solution)/shard_map/all_gather | solution.py:157
  413.0 76.2 %copy-start.1 = (bf16[4,36864]{1,0:T(4,128)(2,1)S(1)}, bf16[4,36864]{1,0:T(4,128)(2,1)}, u32[]{:S(2)}) copy-start(bf16[4,36864]{1,0:T(4,128)(2,1)} %param.4) | copy-start | bytes 884740
Sparse Core Ops, SparseCore 0:
  263.1 147.6 reduce-scatter.1
  413.1 71.5 all-gather.1
where the time goes:
time: 500 us; the launch traced here: 497 us
  waiting for transfers between devices  215 us (43%)
  matrix products  122 us (24%)
  local copies, waits for them, and re-layouts  78.8 us (16%)
  blocking collectives  28.5 us (6%)
  other arithmetic  20.9 us (4%)
  starting transfers between devices  17.7 us (4%)
  between operations  14.5 us (3%)
    reduce_scatter x1, waiting for transfers between devices, shards(): piece = lax.psum_scatter(totals, 'dom', scatter_dimension=1, tiled=True)  125 us
    all_gather x1, waiting for transfers between devices, shards(): return lax.all_gather(average_piece, 'dom', axis=1, tiled=True)  71.7 us
    dot_general x5, matrix products, shards(): jnp.einsum('xjf,clf->xjcl', moved, class_refs, preferred_element_type=jnp...  49.6 us
    dot_general x5, matrix products, shards(): jnp.einsum('xcjl,xjf->clf', spread, moved_list[shift], preferred_element_...  47.6 us
    convert_element_type x5, local copies, waits for them, and re-layouts, shards(): spread = jnp.einsum('xcr,jlr->xcjl', weight, diagonal_bf16, preferred_ele...  44.9 us
    psum x1, blocking collectives, shards(): summed_mass = lax.psum(masses, 'dom')  22.4 us
    dot_general x5, matrix products, shards(): jnp.einsum('xjcl,jlr->xcr', pairs, diagonal_f32, precision=lax.Precision....  19.4 us
    add x2, other arithmetic, shift_images(): real_part * cosine + imag_part * sine  14.2 us
  transfers between devices with their start and end apart: 7, of which 6 were waited for; matrix products, arithmetic and copies ran while one was open for 2% of the time, Pallas kernels for 0%

commit v1 on v0

v1 whole, which is shorter than its diff:
```python
import functools
import math

import jax
import jax.numpy as jnp
import numpy as np
from jax import lax
from jax.experimental import pallas as pl
from jax.experimental.pallas import tpu as pltpu
from jax.sharding import PartitionSpec as P

CYCLES = 128
ANGLES = 144
ROT = 36
SHIFTS = 5
BOX = 256
LANES = 128
SPAN = 40
STEP_ANGLES = ANGLES // ROT
REACH = 8

SOFTMAX_WARMTH = 2.0
PRIOR_MASS = 1.0
NEGATIVE = -1e30
SHIFT_X_STEPS = (0, 1, -1, 0, 0)
SHIFT_Y_STEPS = (0, 0, 0, 1, -1)
META_ROWS = 16
VMEM_LIMIT = 60 * 1024 * 1024


def trig_tables():
    theta = 2.0 * np.pi * np.arange(ANGLES) / ANGLES
    radius = np.arange(1, CYCLES + 1)
    out = np.zeros((4, REACH + 1, STEP_ANGLES, SPAN, CYCLES), np.float32)
    for axis, direction in enumerate((np.cos(theta), np.sin(theta))):
        for t in range(REACH + 1):
            phase = 2.0 * np.pi / BOX * t * direction[:, None] * radius[None, :]
            for part, fn in enumerate((np.cos, np.sin)):
                table = fn(phase).reshape(ROT, STEP_ANGLES, CYCLES).transpose(1, 0, 2)
                out[2 * axis + part, t, :, :ROT] = table[:, ::-1]
    return out.reshape(4, REACH + 1, STEP_ANGLES * SPAN, CYCLES)


def prep_kernel(groups, capacity, local, cand_ref, off_ref, image_ref, out_ref):
    count, listed = cand_ref.shape
    rows = image_ref.shape[1]
    half = listed // 2
    out_ref[:, :, rows:, :] = jnp.zeros((groups, capacity, META_ROWS, LANES), out_ref.dtype)
    cand = [[cand_ref[u, k] for k in range(listed)] for u in range(count)]
    owner = [[lax.div(c, local) for c in row] for row in cand]
    pair = []
    for u in range(count):
        first = owner[u][0]
        second = first
        for k in range(1, listed):
            second = jnp.where(owner[u][k] != first, owner[u][k], second)
        pair.append((first, second))
    lane = lax.broadcasted_iota(jnp.int32, (META_ROWS, LANES), 1)
    for u in range(count):
        rank = []
        for side in range(2):
            value = jnp.int32(0)
            for v in range(u):
                lists = (pair[v][0] == pair[u][side]) | (pair[v][1] == pair[u][side])
                value = value + jnp.where(lists, 1, 0)
            rank.append(value)
        for side in range(2):
            mine, other = pair[u][side], pair[u][1 - side]
            entries = [jnp.int32(1), off_ref[u, 0], off_ref[u, 1], other, rank[1 - side]]
            classes = [jnp.int32(0)] * half
            seen = jnp.int32(0)
            for k in range(listed):
                hit = owner[u][k] == mine
                for j in range(half):
                    classes[j] = jnp.where(hit & (seen == j), cand[u][k] - mine * local, classes[j])
                seen = seen + jnp.where(hit, 1, 0)
            entries += classes
            tile = jnp.zeros((META_ROWS, LANES), jnp.int32)
            for k, value in enumerate(entries):
                tile = jnp.where(lane == k, value, tile)
            out_ref[mine, rank[side], :rows, :] = image_ref[u]
            out_ref[mine, rank[side], rows:, :] = tile.astype(jnp.float32).astype(out_ref.dtype)


def prepare(images, candidates, offsets, groups, local):
    count, rows, _ = images.shape
    capacity = count // 2
    smem = pl.BlockSpec(memory_space=pltpu.SMEM)
    vmem = pl.BlockSpec(memory_space=pltpu.VMEM)
    return pl.pallas_call(
        functools.partial(prep_kernel, groups, capacity, local),
        out_shape=jax.ShapeDtypeStruct((groups, capacity, rows + META_ROWS, LANES), images.dtype),
        in_specs=[smem, smem, vmem],
        out_specs=vmem,
        name="prepare",
    )(candidates, offsets, images)


def load_image(source, rows, raw):
    group = 2 * STEP_ANGLES
    values = source.astype(jnp.float32)
    for block in range(rows // group):
        at = rows - (block + 1) * group
        raw[at : at + group, :] = values[block * group : (block + 1) * group]


def piece(raw, part):
    return raw[pl.ds(part, SPAN, stride=2 * STEP_ANGLES), :]


def axis_phase(table_ref, axis, step, move):
    size = jnp.abs(move)
    sign = jnp.where(move < 0, -1.0, 1.0).astype(jnp.float32)
    at = pl.ds(step * SPAN, SPAN)
    return table_ref[2 * axis, size, at, :], table_ref[2 * axis + 1, size, at, :] * sign


def read_meta(source, meta_vmem, row):
    meta_vmem[pl.ds(row, 1), :] = source.astype(jnp.float32)[0:1, :].astype(jnp.int32)


def score_kernel(
    image_ref, refs_ref, table_ref, weight_ref, stat_ref, raw, moved, picked, sums, meta_vmem, meta, sem
):
    slots = image_ref.shape[0]
    rows = image_ref.shape[1] - META_ROWS
    classes = picked.shape[0] // 48
    raw[...] = jnp.zeros_like(raw)
    moved[...] = jnp.zeros_like(moved)
    picked[...] = jnp.zeros_like(picked)
    sums[...] = jnp.zeros_like(sums)
    for slot in range(slots):
        read_meta(image_ref[slot, rows:, :], meta_vmem, slot)
    copy = pltpu.make_async_copy(meta_vmem, meta, sem)
    copy.start()
    copy.wait()
    lane = lax.broadcasted_iota(jnp.int32, (1, LANES), 1)
    used = SHIFTS * classes

    def one(slot, carry):
        load_image(image_ref[slot, :rows, :], rows, raw)
        filled = meta[slot, 0]
        base_x, base_y = meta[slot, 1], meta[slot, 2]
        for j in range(classes):
            picked[j * 48 : j * 48 + ROT, :] = refs_ref[meta[slot, 5 + j]]
        for step in range(STEP_ANGLES):
            re, im = piece(raw, 2 * step), piece(raw, 2 * step + 1)
            for s in range(SHIFTS):
                cx, sx = axis_phase(table_ref, 0, step, base_x + SHIFT_X_STEPS[s])
                cy, sy = axis_phase(table_ref, 1, step, base_y + SHIFT_Y_STEPS[s])
                cosine = cx * cy - sx * sy
                sine = sx * cy + cx * sy
                left = pl.ds((2 * step) * LANES, LANES)
                right = pl.ds((2 * step + 1) * LANES, LANES)
                pad = jnp.zeros((8, LANES), jnp.float32)
                new_re = jnp.concatenate([re * cosine + im * sine, pad], axis=0)
                new_im = jnp.concatenate([im * cosine - re * sine, pad], axis=0)
                moved[s * LANES : s * LANES + 48, left] = new_re.astype(jnp.bfloat16)
                moved[s * LANES : s * LANES + 48, right] = new_im.astype(jnp.bfloat16)
        pairs = lax.dot_general(
            picked[...], moved[...], (((1,), (1,)), ((), ())), preferred_element_type=jnp.float32
        )
        for s in range(SHIFTS):
            for j in range(classes):
                block = pairs[j * 48 : j * 48 + SPAN, s * LANES : (s + 1) * LANES]
                turned = pltpu.roll(block, 0, 1, stride=1, stride_axis=0)
                sums[pl.ds(s * classes + j, 1), :] = jnp.sum(turned, axis=0, keepdims=True)
        raw_sums = sums[...]
        scores = SOFTMAX_WARMTH * (raw_sums + pltpu.roll(raw_sums, LANES - ROT, 1))
        lanes = lax.broadcasted_iota(jnp.int32, scores.shape, 1)
        lines = lax.broadcasted_iota(jnp.int32, scores.shape, 0)
        valid = (lanes < ROT) & (lines < used) & (filled > 0)
        scores = jnp.where(valid, scores, NEGATIVE)
        peak = jnp.max(jnp.max(scores, axis=0, keepdims=True), axis=1, keepdims=True)
        peak = jnp.where(filled > 0, peak, 0.0)
        weights = jnp.where(valid, jnp.exp(scores - peak), 0.0)
        total = jnp.sum(jnp.sum(weights, axis=0, keepdims=True), axis=1, keepdims=True)
        total = jnp.where(filled > 0, total, 1.0)
        stat_ref[pl.ds(2 * slot, 1), :] = jnp.broadcast_to(peak, (1, LANES))
        stat_ref[pl.ds(2 * slot + 1, 1), :] = jnp.broadcast_to(total, (1, LANES))
        w = [weights[s * classes : (s + 1) * classes] for s in range(SHIFTS)]
        low = w[0] + pltpu.roll(w[1] + w[2], SPAN, 1) + pltpu.roll(w[1] - w[2], 2 * SPAN, 1)
        high = (w[3] + w[4]) + pltpu.roll(w[3] - w[4], SPAN, 1)
        weight_ref[slot, :classes, :] = low
        weight_ref[slot, classes:, :] = high
        return carry

    lax.fori_loop(0, slots, one, 0)


def score(arrived, refs, tables, classes):
    slots, rows, _ = arrived.shape
    vmem = pl.BlockSpec(memory_space=pltpu.VMEM)
    width = refs.shape[2]
    return pl.pallas_call(
        score_kernel,
        out_shape=(
            jax.ShapeDtypeStruct((slots, 2 * classes, LANES), jnp.float32),
            jax.ShapeDtypeStruct((2 * slots, LANES), jnp.float32),
        ),
        in_specs=[vmem, vmem, vmem],
        out_specs=(vmem, vmem),
        scratch_shapes=[
            pltpu.VMEM((2 * STEP_ANGLES * SPAN, LANES), jnp.float32),
            pltpu.VMEM((SHIFTS * LANES, width), jnp.bfloat16),
            pltpu.VMEM((48 * classes, width), jnp.bfloat16),
            pltpu.VMEM((24, LANES), jnp.float32),
            pltpu.VMEM((slots, LANES), jnp.int32),
            pltpu.SMEM((slots, LANES), jnp.int32),
            pltpu.SemaphoreType.DMA,
        ],
        compiler_params=pltpu.CompilerParams(vmem_limit_bytes=VMEM_LIMIT),
        cost_estimate=pl.CostEstimate(flops=10**10, bytes_accessed=10**7, transcendentals=0),
        name="score",
    )(arrived, refs, tables)


def sum_kernel(
    z_size, y_size, wave, *refs
):
    count = z_size * y_size
    image_refs = refs[:count]
    (
        weight_ref, stat_ref, table_ref, place_ref, out_ref,
        images, raw, moved, totals, mass, meta_vmem, meta, image_sem, meta_sem,
    ) = refs[count:]
    slots = image_refs[0].shape[0]
    rows = image_refs[0].shape[1] - META_ROWS
    classes = weight_ref.shape[2] // 2
    local = out_ref.shape[0]
    width = moved.shape[1]
    depth = images.shape[0]
    waves = count // wave
    capacity = slots // stat_ref.shape[0]

    def copies(w):
        return [
            pltpu.make_async_copy(
                image_refs[w * wave + b],
                images.at[w % depth, pl.ds(b * slots, slots)],
                image_sem.at[w % depth, b],
            )
            for b in range(wave)
        ]

    for w in range(min(depth, waves)):
        for copy in copies(w):
            copy.start()
    raw[...] = jnp.zeros_like(raw)
    moved[...] = jnp.zeros_like(moved)
    mass[...] = jnp.zeros_like(mass)
    totals[...] = jnp.zeros_like(totals)
    my_cls, my_z, my_y = place_ref[0], place_ref[1], place_ref[2]
    lane = lax.broadcasted_iota(jnp.int32, (2 * classes, LANES), 1)
    lane_wide = lax.broadcasted_iota(jnp.int32, (SPAN, LANES), 1)

    for w in range(waves):
        for copy in copies(w):
            copy.wait()
        here = images.at[w % depth]
        for i in range(wave * slots):
            read_meta(here[i, rows:, :], meta_vmem, i)
        meta_copy = pltpu.make_async_copy(meta_vmem, meta, meta_sem)
        meta_copy.start()
        meta_copy.wait()

        def one(i, carry):
            b = w * wave + i // slots
            slot = i % slots
            q_z = lax.rem(my_z - lax.rem(b, z_size) + z_size, z_size)
            q_y = lax.rem(my_y - b // z_size + y_size, y_size)
            q = q_z * y_size + q_y
            source = slot // capacity
            other, other_rank = meta[i, 3], meta[i, 4]
            mine = stat_ref[my_cls, q, pl.ds(2 * slot, 2), :]
            theirs = stat_ref[other, q, pl.ds(2 * (source * capacity + other_rank), 2), :]
            peak = jnp.maximum(mine[0:1], theirs[0:1])
            gain = jnp.exp(mine[0:1] - peak)
            factor = gain / (mine[1:2] * gain + theirs[1:2] * jnp.exp(theirs[0:1] - peak))
            weights = weight_ref[q, slot] * factor
            load_image(here[i, :rows, :], rows, raw)
            base_x, base_y = meta[i, 1], meta[i, 2]
            for step in range(STEP_ANGLES):
                re, im = piece(raw, 2 * step), piece(raw, 2 * step + 1)
                cx, sx = axis_phase(table_ref, 0, step, base_x)
                cy, sy = axis_phase(table_ref, 1, step, base_y)
                cosine = cx * cy - sx * sy
                sine = sx * cy + cx * sy
                re, im = re * cosine + im * sine, im * cosine - re * sine
                at = pl.ds(step * SPAN, SPAN)
                c1, s1 = table_ref[0, 1, at, :], table_ref[1, 1, at, :]
                c2, s2 = table_ref[2, 1, at, :], table_ref[3, 1, at, :]
                pad = jnp.zeros((8, LANES), jnp.float32)
                left = pl.ds((2 * step) * LANES, LANES)
                right = pl.ds((2 * step + 1) * LANES, LANES)
                moved[:LANES, left] = jnp.concatenate([re, re * c1, im * s1, pad], axis=0).astype(jnp.bfloat16)
                moved[:LANES, right] = jnp.concatenate([im, im * c1, -re * s1, pad], axis=0).astype(jnp.bfloat16)
                moved[LANES : LANES + 2 * SPAN, left] = jnp.concatenate([re * c2, im * s2], axis=0).astype(jnp.bfloat16)
                moved[LANES : LANES + 2 * SPAN, right] = jnp.concatenate([im * c2, -re * s2], axis=0).astype(
                    jnp.bfloat16
                )
            parts = []
            for k in range(3):
                part = jnp.where((lane >= k * SPAN) & (lane < (k + 1) * SPAN), weights, 0.0)
                parts.append(part + pltpu.roll(part, LANES - ROT, 1))
            blocks = []
            for j in range(classes):
                line = []
                for half in range(2):
                    at = half * classes + j
                    turned = [
                        pltpu.roll(
                            jnp.broadcast_to(parts[k][at : at + 1], (SPAN, LANES)), 1, 1, stride=1, stride_axis=0
                        )
                        for k in range(3 - half)
                    ]
                    tile = jnp.where(lane_wide < SPAN, turned[0], turned[1])
                    if half == 0:
                        tile = jnp.where(lane_wide < 2 * SPAN, tile, turned[2])
                    line.append(tile)
                blocks.append(jnp.concatenate(line, axis=1))
            spread = jnp.concatenate(blocks, axis=0).astype(jnp.bfloat16)
            added = jnp.dot(spread, moved[...], preferred_element_type=jnp.float32)
            plain = jnp.where(lane < 2 * SPAN, weights, 0.0)
            plain_high = jnp.where(lane < SPAN, weights, 0.0)
            for j in range(classes):
                c = meta[i, 5 + j]
                for tile in range(width // LANES):
                    at = pl.ds(pl.multiple_of(tile * local * SPAN + c * SPAN, 8), SPAN)
                    totals[at, :] += added[j * SPAN : (j + 1) * SPAN, tile * LANES : (tile + 1) * LANES]
                mass[pl.ds(c, 1), :] += plain[j : j + 1] + plain_high[classes + j : classes + j + 1]
            return carry

        lax.fori_loop(0, wave * slots, one, 0)
        if w + depth < waves:
            for copy in copies(w + depth):
                copy.start()

    scale = 1.0 / (jnp.sum(mass[:local, :], axis=1, keepdims=True) + PRIOR_MASS)
    for turn in range(ROT):
        for tile in range(width // LANES):
            line = totals[pl.ds(tile * local * SPAN + ROT - 1 - turn, local, stride=SPAN), :]
            out_ref[:, pl.ds(turn * width + tile * LANES, LANES)] = (line * scale).astype(out_ref.dtype)


def class_sum(buffers, weights, stats, tables, place, z_size, y_size, local, width, classes):
    slots, rows, _ = buffers[0].shape
    count = len(buffers)
    wave = math.gcd(count, 8)
    depth = min(2, count // wave)
    vmem = pl.BlockSpec(memory_space=pltpu.VMEM)
    smem = pl.BlockSpec(memory_space=pltpu.SMEM)
    hbm = pl.BlockSpec(memory_space=pl.ANY)
    return pl.pallas_call(
        functools.partial(sum_kernel, z_size, y_size, wave),
        out_shape=jax.ShapeDtypeStruct((local, ROT * width), jnp.bfloat16),
        in_specs=[hbm] * count + [vmem, vmem, vmem, smem],
        out_specs=vmem,
        scratch_shapes=[
            pltpu.VMEM((depth, wave * slots, rows, LANES), jnp.bfloat16),
            pltpu.VMEM((2 * STEP_ANGLES * SPAN, LANES), jnp.float32),
            pltpu.VMEM((2 * LANES, width), jnp.bfloat16),
            pltpu.VMEM((width // LANES * local * SPAN, LANES), jnp.float32),
            pltpu.VMEM((-(-local // 8) * 8, LANES), jnp.float32),
            pltpu.VMEM((wave * slots, LANES), jnp.int32),
            pltpu.SMEM((wave * slots, LANES), jnp.int32),
            pltpu.SemaphoreType.DMA((depth, wave)),
            pltpu.SemaphoreType.DMA,
        ],
        compiler_params=pltpu.CompilerParams(vmem_limit_bytes=VMEM_LIMIT),
        cost_estimate=pl.CostEstimate(flops=2 * 10**10, bytes_accessed=10**7, transcendentals=0),
        name="class_sum",
    )(*buffers, weights, stats, tables, place)


def shards(z_size, y_size, particles, references, candidates, offsets):
    groups = lax.axis_size("cls")
    doms = lax.axis_size("dom")
    count, width = particles.shape
    local = references.shape[0]
    classes = candidates.shape[1] // 2
    block_width = width // ROT
    slots = groups * (count // 2)
    tables = jnp.asarray(trig_tables())
    images = particles.reshape(count, width // LANES, LANES)
    outgoing = prepare(images, candidates, offsets, groups, local)
    arrived = lax.all_to_all(outgoing, "cls", split_axis=0, concat_axis=0, tiled=True)
    arrived = arrived.reshape(slots, width // LANES + META_ROWS, LANES)
    refs = references.reshape(local, ROT, block_width)

    def along(dz, dy):
        return [
            (z * y_size + y, (z + dz) % z_size * y_size + (y + dy) % y_size)
            for z in range(z_size)
            for y in range(y_size)
        ]

    ring = [arrived]
    for _ in range(z_size - 1):
        ring.append(lax.ppermute(ring[-1], "dom", along(1, 0)))
    buffers = list(ring)
    for _ in range(y_size - 1):
        ring = [lax.ppermute(part, "dom", along(0, 1)) for part in ring]
        buffers += ring

    weights, stats = score(arrived, refs, tables, classes)
    weights = lax.all_to_all(
        jnp.broadcast_to(weights[None], (doms, *weights.shape)), "dom", split_axis=0, concat_axis=0, tiled=True
    )
    stats = lax.all_to_all(
        jnp.broadcast_to(stats[None], (groups * doms, *stats.shape)),
        ("cls", "dom"),
        split_axis=0,
        concat_axis=0,
        tiled=True,
    )
    stats = stats.reshape(groups, doms, *stats.shape[1:])
    dom = lax.axis_index("dom")
    place = jnp.stack([lax.axis_index("cls"), dom // y_size, dom % y_size]).astype(jnp.int32)
    return class_sum(buffers, weights, stats, tables, place, z_size, y_size, local, block_width, classes)


def solution(mesh):
    coords = [device.coords for device in mesh.devices.flat]
    z_size = len({c[2] for c in coords})
    y_size = len({c[1] for c in coords})
    in_specs = (
        P(("cls", "dom"), None),
        P("cls", None),
        P(("cls", "dom"), None),
        P(("cls", "dom"), None),
    )
    out_specs = P("cls", None)
    return jax.shard_map(
        functools.partial(shards, z_size, y_size),
        mesh=mesh,
        in_specs=in_specs,
        out_specs=out_specs,
        check_vma=False,
    )
```

time: 500 us -> 174 us (0.35)
  waiting for transfers between devices: 215 us -> 75.4 us
  matrix products: 122 us -> 0 us
  local copies, waits for them, and re-layouts: 78.8 us -> 14.2 us
  Pallas kernels: 0 us -> 54.5 us
  other arithmetic: 20.9 us -> 0.58 us
  between operations: 14.5 us -> 0.09 us
  blocking collectives: 28.5 us -> 14.1 us
    reduce_scatter x1 -> x0, waiting for transfers between devices: 125 us -> none  [shards(): piece = lax.psum_scatter(totals, 'dom', scatter_dimension=1, tiled=True)]
    dot_general x22 -> x0, matrix products: 122 us -> none  [the longest x5 49.6 us: shards(): jnp.einsum('xjf,clf->xjcl', moved, class_refs, preferred_element_type=jnp...]
    all_gather x1 -> x0, waiting for transfers between devices: 71.7 us -> none  [shards(): return lax.all_gather(average_piece, 'dom', axis=1, tiled=True)]
    pallas_call x0 -> x3, Pallas kernels: none -> 54.5 us  [the longest x1 39.3 us: class_sum(): pl.pallas_call(functools.partial(sum_kernel, z_size, y_size, wave), out_s...]
    convert_element_type x17 -> x0, local copies, waits for them, and re-layouts: 52.6 us -> none  [the longest x5 44.9 us: shards(): spread = jnp.einsum('xcr,jlr->xcjl', weight, diagonal_bf16, preferred_ele...]
    all_to_all x5 -> x2, waiting for transfers between devices: 17.6 us -> 50.3 us  [the longest x1 46.1 us: shards(): lax.all_to_all(jnp.broadcast_to(stats[None], (groups * doms, *stats.shape...]
    ppermute x0 -> x7, waiting for transfers between devices: none -> 25.1 us  [the longest x3 25.1 us: shards(): ring.append(lax.ppermute(ring[-1], 'dom', along(1, 0)))]
    psum x1 -> x0, blocking collectives: 22.4 us -> none  [shards(): summed_mass = lax.psum(masses, 'dom')]
  transfers between devices with their start and end apart: 7 -> 9, of which waited for: 6 -> 4; matrix products, arithmetic and copies ran while one was open for 2% -> 6% of each run, Pallas kernels for 0% -> 7%
where the time goes in v1:
time: 174 us
  waiting for transfers between devices  75.4 us (43%)
  Pallas kernels  54.5 us (31%)
  starting transfers between devices  14.6 us (8%)
  local copies, waits for them, and re-layouts  14.2 us (8%)
  blocking collectives  14.1 us (8%)
    all_to_all x1, waiting for transfers between devices, shards(): lax.all_to_all(jnp.broadcast_to(stats[None], (groups * doms, *stats.shape...  46.1 us
    pallas_call x1, Pallas kernels, class_sum(): pl.pallas_call(functools.partial(sum_kernel, z_size, y_size, wave), out_s...  39.3 us
    ppermute x3, waiting for transfers between devices, shards(): ring.append(lax.ppermute(ring[-1], 'dom', along(1, 0)))  25.1 us
    all_to_all x1, blocking collectives, shards(): lax.all_to_all(outgoing, 'cls', split_axis=0, concat_axis=0, tiled=True)  14.1 us
    pallas_call x1, Pallas kernels, score(): pl.pallas_call(score_kernel, out_shape=(jax.ShapeDtypeStruct((slots, 2 *...  12.9 us
    reshape x1, local copies, waits for them, and re-layouts, shards(): refs = references.reshape(local, ROT, block_width)  7.34 us
    all_to_all x1, starting transfers between devices, shards(): lax.all_to_all(jnp.broadcast_to(weights[None], (doms, *weights.shape)), '...  5.58 us
    all_to_all x1, waiting for transfers between devices, shards(): lax.all_to_all(jnp.broadcast_to(weights[None], (doms, *weights.shape)), '...  4.19 us
  transfers between devices with their start and end apart: 9, of which 4 were waited for; matrix products, arithmetic and copies ran while one was open for 6% of the time, Pallas kernels for 7%

profile of v1, /device:TPU:0, one launch (start us, length us, event | category | flops | bytes accessed | tf_op | source)
XLA Modules:
  0.0 173.5 jit_solution(12449706973384282380)
XLA Ops:
  0.0 1.3 copy.6.off_ref
  1.3 1.7 copy.9
  3.1 2.4 %prepare.1 = bf16[4,2,304,128]{3,2,1,0:T(8,128)(2,1)} custom-call(s32[4,8]{1,0:T(4,128)} %cand_ref.1, s32[4,2]{1,0:T(4,128)} %copy.6.off_ref, bf16[4,288,128]{2,1,0:T(8,128)(2,1)} %bitcast.9), custom_call_target="tpu_custom_call" | custom-call | tf_op jit(solution)/shard_map/prepare/pallas_call | solution.py:90
  5.4 14.1 %all_to_all.15 = bf16[4,2,304,128]{3,2,1,0:T(8,128)(2,1)S(1)} all-to-all(bf16[4,2,304,128]{3,2,1,0:T(8,128)(2,1)} %prepare.1), channel_id=1, replica_groups=mesh['cls'=4,'dom'=8] {'cls'}, dimensions={0} | all-to-all | bytes 1245184 | tf_op jit(solution)/shard_map/all_to_all | solution.py:387
  19.5 2.3 %collective-permute-start = (bf16[8,304,128]{2,1,0:T(8,128)(2,1)S(1)}, bf16[8,304,128]{2,1,0:T(8,128)(2,1)S(1)}, u32[]{:S(2)}, u32[]{:S(2)}) collective-permute-start(bf16[8,304,128]{2,1,0:T(8,128)(2,1)S(1)} %bitcast.10), channel_id=1, source_target_pairs={{0,2},{1,3},{2,4},{3,5},{4,6},{5,7},{6,0},{7,1},{8,10},{9,11},{10,... | collective-permute-start | bytes 1867784 | tf_op jit(solution)/shard_map/ppermute | solution.py:400
  21.8 15.8 %collective-permute-done.refs_1_ = bf16[8,304,128]{2,1,0:T(8,128)(2,1)S(1)} collective-permute-done((bf16[8,304,128]{2,1,0:T(8,128)(2,1)S(1)}, bf16[8,304,128]{2,1,0:T(8,128)(2,1)S(1)}, u32[]{:S(2)}, u32[]{:S(2)}) %collective-permute-start) | collective-permute-done | bytes 622624 | tf_op jit(solution)/shard_map/ppermute | solution.py:400
  37.6 0.0 collective-permute-start.1
  37.6 7.3 %reshape.16.refs_ref = bf16[50,36,1024]{2,1,0:T(8,128)(2,1)} reshape(bf16[50,36864]{1,0:T(8,128)(2,1)} %param.6) | data formatting | bytes 7372800 | tf_op jit(solution)/shard_map/reshape | solution.py:389
  44.9 9.4 %collective-permute-done.1.refs_2_ = bf16[8,304,128]{2,1,0:T(8,128)(2,1)S(1)} collective-permute-done((bf16[8,304,128]{2,1,0:T(8,128)(2,1)S(1)}, bf16[8,304,128]{2,1,0:T(8,128)(2,1)S(1)}, u32[]{:S(2)}, u32[]{:S(2)}) %collective-permute-start.1) | collective-permute-done | bytes 622624 | tf_op jit(solution)/shard_map/ppermute | solution.py:400
  54.3 0.0 collective-permute-start.2
  54.3 0.0 copy-done
  54.3 12.9 %score.1 = (f32[8,8,128]{2,1,0:T(8,128)}, f32[16,128]{1,0:T(8,128)}) custom-call(bf16[8,304,128]{2,1,0:T(8,128)(2,1)} %bitcast.11, bf16[50,36,1024]{2,1,0:T(8,128)(2,1)} %reshape.16.refs_ref, f32[4,9,160,128]{3,2,1,0:T(8,128)} %constant.34.clone.table_ref.refs_10_), custom_call_target="tpu_custom_call" | custom-call | flops 10000000000 | bytes 10000000 | tf_op jit(solution)/shard_map/score/pallas_call | solution.py:195
  67.2 1.5 broadcast_in_dim.4
  68.7 5.6 %all-to-all-start.1 = ((f32[8,8,8,128]{3,2,1,0:T(8,128)}), f32[8,8,8,128]{3,2,1,0:T(8,128)S(1)}, u32[]{:S(2)}, u32[]{:S(2)}) async-start(f32[8,8,8,128]{3,2,1,0:T(8,128)} %broadcast_in_dim.4), calls=%async_computation.1 | async-start | bytes 524288 | tf_op jit(solution)/shard_map/all_to_all | solution.py:407
  74.2 2.0 %collective-permute-start.3 = (bf16[8,304,128]{2,1,0:T(8,128)(2,1)}, bf16[8,304,128]{2,1,0:T(8,128)(2,1)S(1)}, u32[]{:S(2)}, u32[]{:S(2)}) collective-permute-start(bf16[8,304,128]{2,1,0:T(8,128)(2,1)} %bitcast.12), channel_id=1, source_target_pairs={{0,1},{1,0},{2,3},{3,2},{4,5},{5,4},{6,7},{7,6},{8,9},{9,8},{10,11... | collective-permute-start | bytes 1867784 | tf_op jit(solution)/shard_map/ppermute | solution.py:403
  76.3 0.0 copy-done.3
  76.3 0.1 collective-permute-start.4
  76.3 2.0 %collective-permute-start.5 = (bf16[8,304,128]{2,1,0:T(8,128)(2,1)S(1)}, bf16[8,304,128]{2,1,0:T(8,128)(2,1)}, u32[]{:S(2)}, u32[]{:S(2)}) collective-permute-start(bf16[8,304,128]{2,1,0:T(8,128)(2,1)S(1)} %collective-permute-done.1.refs_2_), channel_id=1, source_target_pairs={{0,1},{1,0},{2,3},{3,2},{4,5},{5,4},{6,7},{7,6},{8,9},{9,8},{10,11... | collective-permute-start | bytes 1867784 | tf_op jit(solution)/shard_map/ppermute | solution.py:403
  78.3 0.0 collective-permute-done.2.refs_3_
  78.3 0.1 collective-permute-start.6
  78.4 4.2 %all-to-all-done.1.refs_8_ = f32[8,8,8,128]{3,2,1,0:T(8,128)S(1)} async-done(((f32[8,8,8,128]{3,2,1,0:T(8,128)}), f32[8,8,8,128]{3,2,1,0:T(8,128)S(1)}, u32[]{:S(2)}, u32[]{:S(2)}) %all-to-all-start.1) | async-done | bytes 262176 | tf_op jit(solution)/shard_map/all_to_all | solution.py:407
  82.6 1.4 broadcast_in_dim.5
  84.0 2.6 %all-to-all-start.2 = ((f32[32,16,128]{2,1,0:T(8,128)}), f32[32,16,128]{2,1,0:T(8,128)S(1)}, u32[]{:S(2)}, u32[]{:S(2)}) async-start(f32[32,16,128]{2,1,0:T(8,128)} %broadcast_in_dim.5), calls=%async_computation.2 | async-start | bytes 524288 | tf_op jit(solution)/shard_map/all_to_all | solution.py:410
  86.6 0.6 pad_add_fusion.refs_11_
  87.2 46.1 %all-to-all-done.2 = f32[32,16,128]{2,1,0:T(8,128)S(1)} async-done(((f32[32,16,128]{2,1,0:T(8,128)}), f32[32,16,128]{2,1,0:T(8,128)S(1)}, u32[]{:S(2)}, u32[]{:S(2)}) %all-to-all-start.2) | async-done | bytes 262176 | tf_op jit(solution)/shard_map/all_to_all | solution.py:410
  133.3 0.0 collective-permute-done.3.refs_4_
  133.3 0.0 collective-permute-done.4.refs_5_
  133.3 0.0 collective-permute-done.5.refs_6_
  133.3 0.0 collective-permute-done.6.refs_7_
  133.3 0.7 copy-done.2
  134.0 0.3 copy-done.6
  134.2 39.3 %class_sum.1 = bf16[50,36864]{1,0:T(8,128)(2,1)} custom-call(bf16[8,304,128]{2,1,0:T(8,128)(2,1)} %bitcast.13, bf16[8,304,128]{2,1,0:T(8,128)(2,1)} %copy-done.3, bf16[8,304,128]{2,1,0:T(8,128)(2,1)} %copy-done.4, bf16[8,304,128]{2,1,0:T(8,128)(2,1)} %copy-done.5, bf16[8,304,128]{2,1,0:T(8,128)(2,1)} %copy-done.6, ...), custom_call_target="tpu_custom_call" | custom-call | flops 20000000000 | bytes 10000000 | tf_op jit(solution)/shard_map/class_sum/pallas_call | solution.py:354
  (10 shorter events, 0.0 us)
Async XLA Ops:
  19.5 34.7 %copy-start = (bf16[4,2,304,128]{3,2,1,0:T(8,128)(2,1)}, bf16[4,2,304,128]{3,2,1,0:T(8,128)(2,1)S(1)}, u32[]{:S(2)}) copy-start(bf16[4,2,304,128]{3,2,1,0:T(8,128)(2,1)S(1)} %all_to_all.15) | copy-start | bytes 1867780
  19.5 18.0 %collective-permute-start = (bf16[8,304,128]{2,1,0:T(8,128)(2,1)S(1)}, bf16[8,304,128]{2,1,0:T(8,128)(2,1)S(1)}, u32[]{:S(2)}, u32[]{:S(2)}) collective-permute-start(bf16[8,304,128]{2,1,0:T(8,128)(2,1)S(1)} %bitcast.10), channel_id=1, source_target_pairs={{0,2},{1,3},{2,4},{3,5},{4,6},{5,7},{6,0},{7,1},{8,10},{9,11},{10,... | collective-permute-start | bytes 1867784 | tf_op jit(solution)/shard_map/ppermute | solution.py:400
  37.6 38.7 %copy-start.3 = (bf16[8,304,128]{2,1,0:T(8,128)(2,1)}, bf16[8,304,128]{2,1,0:T(8,128)(2,1)S(1)}, u32[]{:S(2)}) copy-start(bf16[8,304,128]{2,1,0:T(8,128)(2,1)S(1)} %collective-permute-done.refs_1_) | copy-start | bytes 1867780
  37.6 16.7 %collective-permute-start.1 = (bf16[8,304,128]{2,1,0:T(8,128)(2,1)S(1)}, bf16[8,304,128]{2,1,0:T(8,128)(2,1)S(1)}, u32[]{:S(2)}, u32[]{:S(2)}) collective-permute-start(bf16[8,304,128]{2,1,0:T(8,128)(2,1)S(1)} %collective-permute-done.refs_1_), channel_id=1, source_target_pairs={{0,2},{1,3},{2,4},{3,5},{4,6},{5,7},{6,0},{7,1},{8,10},{9,11},{10,... | collective-permute-start | bytes 1867784 | tf_op jit(solution)/shard_map/ppermute | solution.py:400
  54.3 22.1 %copy-start.4 = (bf16[8,304,128]{2,1,0:T(8,128)(2,1)}, bf16[8,304,128]{2,1,0:T(8,128)(2,1)S(1)}, u32[]{:S(2)}) copy-start(bf16[8,304,128]{2,1,0:T(8,128)(2,1)S(1)} %collective-permute-done.1.refs_2_) | copy-start | bytes 1867780
  54.3 24.0 %collective-permute-start.2 = (bf16[8,304,128]{2,1,0:T(8,128)(2,1)S(1)}, bf16[8,304,128]{2,1,0:T(8,128)(2,1)S(1)}, u32[]{:S(2)}, u32[]{:S(2)}) collective-permute-start(bf16[8,304,128]{2,1,0:T(8,128)(2,1)S(1)} %collective-permute-done.1.refs_2_), channel_id=1, source_target_pairs={{0,2},{1,3},{2,4},{3,5},{4,6},{5,7},{6,0},{7,1},{8,10},{9,11},{10,... | collective-permute-start | bytes 1867784 | tf_op jit(solution)/shard_map/ppermute | solution.py:400
  68.7 13.9 %all-to-all-start.1 = ((f32[8,8,8,128]{3,2,1,0:T(8,128)}), f32[8,8,8,128]{3,2,1,0:T(8,128)S(1)}, u32[]{:S(2)}, u32[]{:S(2)}) async-start(f32[8,8,8,128]{3,2,1,0:T(8,128)} %broadcast_in_dim.4), calls=%async_computation.1 | async-start | bytes 524288 | tf_op jit(solution)/shard_map/all_to_all | solution.py:407
  74.2 59.0 %collective-permute-start.3 = (bf16[8,304,128]{2,1,0:T(8,128)(2,1)}, bf16[8,304,128]{2,1,0:T(8,128)(2,1)S(1)}, u32[]{:S(2)}, u32[]{:S(2)}) collective-permute-start(bf16[8,304,128]{2,1,0:T(8,128)(2,1)} %bitcast.12), channel_id=1, source_target_pairs={{0,1},{1,0},{2,3},{3,2},{4,5},{5,4},{6,7},{7,6},{8,9},{9,8},{10,11... | collective-permute-start | bytes 1867784 | tf_op jit(solution)/shard_map/ppermute | solution.py:403
  76.3 57.0 %collective-permute-start.4 = (bf16[8,304,128]{2,1,0:T(8,128)(2,1)S(1)}, bf16[8,304,128]{2,1,0:T(8,128)(2,1)}, u32[]{:S(2)}, u32[]{:S(2)}) collective-permute-start(bf16[8,304,128]{2,1,0:T(8,128)(2,1)S(1)} %collective-permute-done.refs_1_), channel_id=1, source_target_pairs={{0,1},{1,0},{2,3},{3,2},{4,5},{5,4},{6,7},{7,6},{8,9},{9,8},{10,11... | collective-permute-start | bytes 1867784 | tf_op jit(solution)/shard_map/ppermute | solution.py:403
  76.3 56.9 %collective-permute-start.5 = (bf16[8,304,128]{2,1,0:T(8,128)(2,1)S(1)}, bf16[8,304,128]{2,1,0:T(8,128)(2,1)}, u32[]{:S(2)}, u32[]{:S(2)}) collective-permute-start(bf16[8,304,128]{2,1,0:T(8,128)(2,1)S(1)} %collective-permute-done.1.refs_2_), channel_id=1, source_target_pairs={{0,1},{1,0},{2,3},{3,2},{4,5},{5,4},{6,7},{7,6},{8,9},{9,8},{10,11... | collective-permute-start | bytes 1867784 | tf_op jit(solution)/shard_map/ppermute | solution.py:403
  78.3 55.0 %copy-start.5 = (bf16[8,304,128]{2,1,0:T(8,128)(2,1)}, bf16[8,304,128]{2,1,0:T(8,128)(2,1)S(1)}, u32[]{:S(2)}) copy-start(bf16[8,304,128]{2,1,0:T(8,128)(2,1)S(1)} %collective-permute-done.2.refs_3_) | copy-start | bytes 1867780
  78.3 55.0 %collective-permute-start.6 = (bf16[8,304,128]{2,1,0:T(8,128)(2,1)S(1)}, bf16[8,304,128]{2,1,0:T(8,128)(2,1)}, u32[]{:S(2)}, u32[]{:S(2)}) collective-permute-start(bf16[8,304,128]{2,1,0:T(8,128)(2,1)S(1)} %collective-permute-done.2.refs_3_), channel_id=1, source_target_pairs={{0,1},{1,0},{2,3},{3,2},{4,5},{5,4},{6,7},{7,6},{8,9},{9,8},{10,11... | collective-permute-start | bytes 1867784 | tf_op jit(solution)/shard_map/ppermute | solution.py:403
  82.6 50.7 %copy-start.1 = (f32[8,8,8,128]{3,2,1,0:T(8,128)}, f32[8,8,8,128]{3,2,1,0:T(8,128)S(1)}, u32[]{:S(2)}) copy-start(f32[8,8,8,128]{3,2,1,0:T(8,128)S(1)} %all-to-all-done.1.refs_8_) | copy-start | bytes 786436
  84.0 49.3 %all-to-all-start.2 = ((f32[32,16,128]{2,1,0:T(8,128)}), f32[32,16,128]{2,1,0:T(8,128)S(1)}, u32[]{:S(2)}, u32[]{:S(2)}) async-start(f32[32,16,128]{2,1,0:T(8,128)} %broadcast_in_dim.5), calls=%async_computation.2 | async-start | bytes 524288 | tf_op jit(solution)/shard_map/all_to_all | solution.py:410
  133.3 0.7 copy-start.2
  133.3 1.0 copy-start.6

commit v2 on v1

v2 whole, which is shorter than its diff:
```python
import functools
import math

import jax
import jax.numpy as jnp
import numpy as np
from jax import lax
from jax.experimental import pallas as pl
from jax.experimental.pallas import tpu as pltpu
from jax.sharding import PartitionSpec as P

CYCLES = 128
ANGLES = 144
ROT = 36
SHIFTS = 5
BOX = 256
LANES = 128
SPAN = 40
STEP_ANGLES = ANGLES // ROT
PIECES = 2 * STEP_ANGLES
IMAGE_ROWS = PIECES * SPAN
REACH = 7

SOFTMAX_WARMTH = 2.0
PRIOR_MASS = 1.0
NEGATIVE = -1e30
META_ROWS = 16
VMEM_LIMIT = 60 * 1024 * 1024
DOM, OWNER, SLOT, CLASS = 0, 1, 3, 5
FILLED, OTHER, OTHER_SLOT = 0, 1, 2


def trig_tables():
    theta = 2.0 * np.pi * np.arange(ANGLES) / ANGLES
    radius = np.arange(1, CYCLES + 1)
    out = np.zeros((4, REACH + 1, STEP_ANGLES, SPAN, CYCLES), np.float32)
    for axis, direction in enumerate((np.cos(theta), np.sin(theta))):
        for t in range(REACH + 1):
            phase = 2.0 * np.pi / BOX * t * direction[:, None] * radius[None, :]
            for part, fn in enumerate((np.cos, np.sin)):
                table = fn(phase).reshape(ROT, STEP_ANGLES, CYCLES).transpose(1, 0, 2)
                out[2 * axis + part, t, :, :ROT] = table[:, ::-1]
    return out.reshape(4, REACH + 1, STEP_ANGLES * SPAN, CYCLES)


def axis_phase(table_ref, axis, step, move):
    size = jnp.abs(move)
    sign = jnp.where(move < 0, -1.0, 1.0).astype(jnp.float32)
    at = pl.ds(step * SPAN, SPAN)
    return table_ref[2 * axis, size, at, :], table_ref[2 * axis + 1, size, at, :] * sign


def prep_kernel(local, place_ref, near_ref, far_ref, image_near, image_far, table_ref, mine_ref, rest_ref, raw):
    count = near_ref.shape[0]
    listed = near_ref.shape[1] - 2
    rows = image_near.shape[1]
    half = listed // 2
    share = count // 2
    my_cls, my_dom = place_ref[0], place_ref[1]
    core = lax.rem(my_cls, 2)
    raw[...] = jnp.zeros_like(raw)
    lane = lax.broadcasted_iota(jnp.int32, (META_ROWS, LANES), 1)
    for far in range(2):
        record, image_ref = (far_ref, image_far) if far else (near_ref, image_near)
        source_core = 1 - core if far else core
        source = my_cls - core + source_core
        cand = [[record[u, k] for k in range(listed)] for u in range(count)]
        owner = [[lax.div(c, local) for c in row] for row in cand]
        pair = []
        for u in range(count):
            first = owner[u][0]
            second = first
            for k in range(1, listed):
                second = jnp.where(owner[u][k] != first, owner[u][k], second)
            pair.append((first, second))
        for u in range(count):
            entries = [my_dom, pair[u][0], pair[u][1]]
            for side in range(2):
                value = source * (count // 2)
                for v in range(u):
                    lists = (pair[v][0] == pair[u][side]) | (pair[v][1] == pair[u][side])
                    value = value + jnp.where(lists, 1, 0)
                entries.append(value)
            for side in range(2):
                classes = [jnp.int32(0)] * half
                seen = jnp.int32(0)
                for k in range(listed):
                    hit = owner[u][k] == pair[u][side]
                    for j in range(half):
                        classes[j] = jnp.where(hit & (seen == j), cand[u][k] - pair[u][side] * local, classes[j])
                    seen = seen + jnp.where(hit, 1, 0)
                entries += classes
            tile = jnp.zeros((META_ROWS, LANES), jnp.int32)
            for k, value in enumerate(entries):
                tile = jnp.where(lane == k, value, tile)
            values = image_ref[u].astype(jnp.float32)
            for block in range(rows // PIECES):
                at = rows - (block + 1) * PIECES
                raw[at : at + PIECES, :] = values[block * PIECES : (block + 1) * PIECES]
            moved = []
            for step in range(STEP_ANGLES):
                re = raw[pl.ds(2 * step, SPAN, stride=PIECES), :]
                im = raw[pl.ds(2 * step + 1, SPAN, stride=PIECES), :]
                cx, sx = axis_phase(table_ref, 0, step, record[u, listed])
                cy, sy = axis_phase(table_ref, 1, step, record[u, listed + 1])
                cosine = cx * cy - sx * sy
                sine = sx * cy + cx * sy
                moved += [re * cosine + im * sine, im * cosine - re * sine]
            moved = jnp.concatenate(moved, axis=0).astype(mine_ref.dtype)
            tile = tile.astype(jnp.float32).astype(mine_ref.dtype)
            at = source_core * share + u % share
            role = u // share

            @pl.when(core == role)
            def _():
                mine_ref[at, :IMAGE_ROWS, :] = moved
                mine_ref[at, IMAGE_ROWS:, :] = tile

            @pl.when(core != role)
            def _():
                rest_ref[at, :IMAGE_ROWS, :] = moved
                rest_ref[at, IMAGE_ROWS:, :] = tile


SMEM_SPEC = pl.BlockSpec(memory_space=pltpu.SMEM)
VMEM_SPEC = pl.BlockSpec(memory_space=pltpu.VMEM)
HBM_SPEC = pl.BlockSpec(memory_space=pl.ANY)


def prepare(place, near, far, image_near, image_far, tables, local):
    count = near.shape[0]
    shape = jax.ShapeDtypeStruct((count, IMAGE_ROWS + META_ROWS, LANES), image_near.dtype)
    return pl.pallas_call(
        functools.partial(prep_kernel, local),
        out_shape=(shape, shape),
        in_specs=[SMEM_SPEC] * 3 + [VMEM_SPEC] * 3,
        out_specs=(VMEM_SPEC, VMEM_SPEC),
        scratch_shapes=[pltpu.VMEM((IMAGE_ROWS, LANES), jnp.float32)],
        compiler_params=pltpu.CompilerParams(vmem_limit_bytes=VMEM_LIMIT),
        name="prepare",
    )(place, near, far, image_near, image_far, tables)


def read_meta(source, meta_vmem, row):
    meta_vmem[pl.ds(row, 1), :] = source.astype(jnp.float32)[0:1, :].astype(jnp.int32)


def move_metas(meta_vmem, meta, sem):
    copy = pltpu.make_async_copy(meta_vmem, meta, sem)
    copy.start()
    copy.wait()


def side_of(meta, i, my_cls):
    return jnp.where(meta[i, OWNER] == my_cls, 0, 1)


def collect(meta, active, total, my_cls):
    def look(i, n):
        mine = (meta[i, OWNER] == my_cls) | (meta[i, OWNER + 1] == my_cls)
        active[n] = i
        return n + jnp.where(mine, 1, 0)

    return lax.fori_loop(0, total, look, jnp.int32(0))


def step_pieces(values, table_ref, step):
    re = values[2 * step * SPAN : (2 * step + 1) * SPAN]
    im = values[(2 * step + 1) * SPAN : (2 * step + 2) * SPAN]
    at = pl.ds(step * SPAN, SPAN)
    return re, im, [table_ref[k, 1, at, :] for k in range(4)]


def store_moved(moved, step, part, blocks):
    at = pl.ds((2 * step + part) * LANES, LANES)
    pad = jnp.zeros((8, LANES), jnp.float32)
    moved[:LANES, at] = jnp.concatenate([*blocks[:3], pad], axis=0).astype(jnp.bfloat16)
    moved[LANES : LANES + 2 * SPAN, at] = jnp.concatenate(blocks[3:], axis=0).astype(jnp.bfloat16)


def score_kernel(count, place_ref, *refs):
    image_refs = refs[:count]
    (
        refs_ref, table_ref, weight_ref, stat_ref, partner_ref,
        moved, picked, sums, meta_vmem, meta, sem,
    ) = refs[count:]
    block = image_refs[0].shape[0]
    slots = weight_ref.shape[0]
    classes = picked.shape[0] // 48
    my_cls, my_dom = place_ref[0], place_ref[1]
    moved[...] = jnp.zeros_like(moved)
    picked[...] = jnp.zeros_like(picked)
    weight_ref[...] = jnp.zeros_like(weight_ref)
    stat_ref[...] = jnp.zeros_like(stat_ref)
    sums[...] = jnp.zeros_like(sums)
    for b in range(count):
        for i in range(block):
            read_meta(image_refs[b][i, IMAGE_ROWS:, :], meta_vmem, b * block + i)
    move_metas(meta_vmem, meta, sem)
    for slot in range(slots):
        for k in range(3):
            partner_ref[slot, k] = 0
    lane = lax.broadcasted_iota(jnp.int32, (SPAN, LANES), 1)

    def one(b, i):
        side = side_of(meta, b * block + i, my_cls)
        index = b * block + i
        slot = meta[index, SLOT + side]
        partner_ref[slot, FILLED] = 1
        partner_ref[slot, OTHER] = meta[index, OWNER + 1 - side]
        partner_ref[slot, OTHER_SLOT] = meta[index, SLOT + 1 - side]
        for j in range(classes):
            picked[j * 48 : j * 48 + ROT, :] = refs_ref[meta[index, CLASS + side * classes + j]]
        values = image_refs[b][i, :IMAGE_ROWS, :].astype(jnp.float32)
        for step in range(STEP_ANGLES):
            re, im, (c1, s1, c2, s2) = step_pieces(values, table_ref, step)
            a1, b1, d1, e1 = re * c1, im * s1, im * c1, re * s1
            a2, b2, d2, e2 = re * c2, im * s2, im * c2, re * s2
            store_moved(moved, step, 0, [re, a1 + b1, a1 - b1, a2 + b2, a2 - b2])
            store_moved(moved, step, 1, [im, d1 - e1, d1 + e1, d2 - e2, d2 + e2])
        pairs = lax.dot_general(
            picked[...], moved[...], (((1,), (1,)), ((), ())), preferred_element_type=jnp.float32
        )
        for s in range(SHIFTS):
            half, k = divmod(s, 3)
            for j in range(classes):
                part = pairs[j * 48 : j * 48 + SPAN, half * LANES : (half + 1) * LANES]
                part = jnp.where((lane >= k * SPAN) & (lane < (k + 1) * SPAN), part, 0.0)
                turned = pltpu.roll(part, 0, 1, stride=1, stride_axis=0)
                sums[k, pl.ds(half * classes + j, 1), :] = jnp.sum(turned, axis=0, keepdims=True)
        found = []
        for k in range(3):
            plain = pltpu.roll(sums[k], (LANES - k * SPAN) % LANES, 1) if k else sums[k]
            found.append(SOFTMAX_WARMTH * (plain + pltpu.roll(plain, LANES - ROT, 1)))
        lanes = lax.broadcasted_iota(jnp.int32, found[0].shape, 1)
        lines = lax.broadcasted_iota(jnp.int32, found[0].shape, 0)
        valid = [lanes < ROT, lanes < ROT, (lanes < ROT) & (lines < classes)]
        found = [jnp.where(v, f, NEGATIVE) for v, f in zip(valid, found)]
        peak = jnp.maximum(jnp.maximum(found[0], found[1]), found[2])
        peak = jnp.max(jnp.max(peak, axis=0, keepdims=True), axis=1, keepdims=True)
        w = [jnp.where(v, jnp.exp(f - peak), 0.0) for v, f in zip(valid, found)]
        total = w[0] + w[1] + w[2]
        total = jnp.sum(jnp.sum(total, axis=0, keepdims=True), axis=1, keepdims=True)
        stat_ref[pl.ds(2 * slot, 1), :] = jnp.broadcast_to(peak, (1, LANES))
        stat_ref[pl.ds(2 * slot + 1, 1), :] = jnp.broadcast_to(total, (1, LANES))
        upper = lines < classes
        first = jnp.where(upper, w[0], w[0] + w[1])
        second = jnp.where(upper, w[1] + w[2], w[0] - w[1])
        third = w[1] - w[2]
        third = jnp.where(upper, third, 0.0)
        weight_ref[slot] = first + pltpu.roll(second, SPAN, 1) + pltpu.roll(third, 2 * SPAN, 1)

    for b in range(count):

        def body(i, carry, b=b):
            @pl.when(
                (meta[b * block + i, DOM] == my_dom)
                & ((meta[b * block + i, OWNER] == my_cls) | (meta[b * block + i, OWNER + 1] == my_cls))
            )
            def _():
                one(b, i)

            return carry

        lax.fori_loop(0, block, body, 0)


def score(place, buffers, refs, tables, slots, classes):
    count, block = len(buffers), buffers[0].shape[0]
    width = refs.shape[2]
    return pl.pallas_call(
        functools.partial(score_kernel, count),
        out_shape=(
            jax.ShapeDtypeStruct((slots, 2 * classes, LANES), jnp.float32),
            jax.ShapeDtypeStruct((2 * slots, LANES), jnp.float32),
            jax.ShapeDtypeStruct((slots, 3), jnp.int32),
        ),
        in_specs=[SMEM_SPEC] + [VMEM_SPEC] * (count + 2),
        out_specs=(VMEM_SPEC, VMEM_SPEC, SMEM_SPEC),
        scratch_shapes=[
            pltpu.VMEM((2 * LANES, width), jnp.bfloat16),
            pltpu.VMEM((48 * classes, width), jnp.bfloat16),
            pltpu.VMEM((3, 2 * classes, LANES), jnp.float32),
            pltpu.VMEM((count * block, LANES), jnp.int32),
            pltpu.SMEM((count * block, LANES), jnp.int32),
            pltpu.SemaphoreType.DMA,
        ],
        compiler_params=pltpu.CompilerParams(vmem_limit_bytes=VMEM_LIMIT),
        cost_estimate=pl.CostEstimate(flops=10**10, bytes_accessed=10**7, transcendentals=0),
        name="score",
    )(place, *buffers, refs, tables)


def weight_kernel(flip, place_ref, partner_ref, weight_ref, *refs):
    stat_refs, out_ref = refs[:-1], refs[-1]
    slots, lines, _ = weight_ref.shape
    my_cls = place_ref[0]
    done = []
    for slot in range(slots):
        other, other_slot = partner_ref[slot, OTHER], partner_ref[slot, OTHER_SLOT]
        at = pl.ds(2 * other_slot, 2)
        if flip:
            mine = stat_refs[0][2 * slot : 2 * slot + 2, :]
            theirs = mine
            for k in range(1, len(stat_refs)):
                theirs = jnp.where(jnp.bitwise_xor(other, my_cls) == k, stat_refs[k][at, :], theirs)
        else:
            mine = stat_refs[0][my_cls, 2 * slot : 2 * slot + 2, :]
            theirs = stat_refs[0][other, at, :]
        peak = jnp.maximum(mine[0:1], theirs[0:1])
        gain = jnp.exp(mine[0:1] - peak)
        mass = mine[1:2] * gain + theirs[1:2] * jnp.exp(theirs[0:1] - peak)
        factor = gain / jnp.where(partner_ref[slot, FILLED] > 0, mass, 1.0)
        done.append(weight_ref[slot] * factor)
    out_ref[...] = jnp.concatenate(done, axis=0).astype(out_ref.dtype)


def normalise(flip, place, partners, weights, stats):
    slots, lines, _ = weights.shape
    return pl.pallas_call(
        functools.partial(weight_kernel, flip),
        out_shape=jax.ShapeDtypeStruct((slots * lines, LANES), jnp.bfloat16),
        in_specs=[SMEM_SPEC] * 2 + [VMEM_SPEC] * (1 + len(stats)),
        out_specs=VMEM_SPEC,
        name="normalise",
    )(place, partners, weights, *stats)


def sum_kernel(relative, z_size, y_size, lines, count, n_weights, place_ref, *refs):
    image_refs = refs[:count]
    weight_refs = refs[count : count + n_weights]
    (
        table_ref, out_ref, images, weights, moved, totals, mass, meta_vmem, meta, active, image_sem, meta_sem,
    ) = refs[count + n_weights :]
    local = out_ref.shape[0]
    width = moved.shape[2]
    depth, wave = images.shape[0], images.shape[1]
    size = image_refs[0].shape[0]
    per_row = weight_refs[0].shape[0]
    classes = lines // 2
    waves = count * size // wave

    def copies(w):
        if size <= wave:
            each = wave // size
            return [
                pltpu.make_async_copy(
                    image_refs[w * each + b], images.at[w % depth, pl.ds(b * size, size)], image_sem.at[w % depth, b]
                )
                for b in range(each)
            ]
        return [
            pltpu.make_async_copy(
                image_refs[0].at[pl.ds(w * wave, wave)], images.at[w % depth], image_sem.at[w % depth, 0]
            )
        ]

    for w in range(min(depth, waves)):
        for copy in copies(w):
            copy.start()
    moved[...] = jnp.zeros_like(moved)
    mass[...] = jnp.zeros_like(mass)
    totals[...] = jnp.zeros_like(totals)
    for b in range(n_weights):
        weights[b * per_row : (b + 1) * per_row, :] = weight_refs[b][...].astype(jnp.float32)
    my_cls, my_dom = place_ref[0], place_ref[1]
    my_z, my_y = lax.div(my_dom, y_size), lax.rem(my_dom, y_size)
    lane = lax.broadcasted_iota(jnp.int32, (lines, LANES), 1)
    lane_wide = lax.broadcasted_iota(jnp.int32, (SPAN, LANES), 1)

    for w in range(waves):
        for copy in copies(w):
            copy.wait()
        here = images.at[w % depth]
        for i in range(wave):
            read_meta(here[i, IMAGE_ROWS:, :], meta_vmem, i)
        move_metas(meta_vmem, meta, meta_sem)
        number = collect(meta, active, wave, my_cls)

        def prepare_one(i, share, buffer):
            side = side_of(meta, i, my_cls)
            q = meta[i, DOM]
            if relative:
                d_z = lax.rem(my_z - lax.div(q, y_size) + z_size, z_size)
                d_y = lax.rem(my_y - lax.rem(q, y_size) + y_size, y_size)
                q = d_y * z_size + d_z
            at = pl.multiple_of(q * per_row + meta[i, SLOT + side] * lines, lines)
            mine = weights[pl.ds(at, lines), :] * share
            values = here[i, :IMAGE_ROWS, :].astype(jnp.float32)
            for step in range(STEP_ANGLES):
                re, im, (c1, s1, c2, s2) = step_pieces(values, table_ref, step)
                store_moved(moved.at[buffer], step, 0, [re, re * c1, im * s1, re * c2, im * s2])
                store_moved(moved.at[buffer], step, 1, [im, im * c1, -re * s1, im * c2, -re * s2])
            parts = []
            for k in range(3):
                part = jnp.where((lane >= k * SPAN) & (lane < (k + 1) * SPAN), mine, 0.0)
                parts.append(part + pltpu.roll(part, LANES - ROT, 1))
            blocks = []
            for j in range(classes):
                line = []
                for half in range(2):
                    at = half * classes + j
                    turned = [
                        pltpu.roll(
                            jnp.broadcast_to(parts[k][at : at + 1], (SPAN, LANES)), 1, 1, stride=1, stride_axis=0
                        )
                        for k in range(3 - half)
                    ]
                    tile = jnp.where(lane_wide < SPAN, turned[0], turned[1])
                    if half == 0:
                        tile = jnp.where(lane_wide < 2 * SPAN, tile, turned[2])
                    line.append(tile)
                blocks.append(jnp.concatenate(line, axis=1))
            spread = jnp.concatenate(blocks, axis=0).astype(jnp.bfloat16)
            plain = jnp.where(lane < 2 * SPAN, mine, 0.0)
            plain_high = jnp.where(lane < SPAN, mine, 0.0)
            masses = [plain[j : j + 1] + plain_high[classes + j : classes + j + 1] for j in range(classes)]
            chosen = [meta[i, CLASS + side * classes + j] for j in range(classes)]
            return spread, masses, chosen

        def add_one(added, masses, chosen):
            for j in range(classes):
                c = chosen[j]
                for tile in range(width // LANES):
                    at = pl.ds(pl.multiple_of(tile * local * SPAN + c * SPAN, 8), SPAN)
                    totals[at, :] += added[j * SPAN : (j + 1) * SPAN, tile * LANES : (tile + 1) * LANES]
                mass[pl.ds(c, 1), :] += masses[j]

        def two(step, carry):
            first = active[2 * step]
            second_at = 2 * step + 1
            second = active[jnp.minimum(second_at, number - 1)]
            share = jnp.where(second_at < number, 1.0, 0.0).astype(jnp.float32)
            one_spread, one_mass, one_chosen = prepare_one(first, 1.0, 0)
            two_spread, two_mass, two_chosen = prepare_one(second, share, 1)
            one_added = jnp.dot(one_spread, moved[0], preferred_element_type=jnp.float32)
            two_added = jnp.dot(two_spread, moved[1], preferred_element_type=jnp.float32)
            add_one(one_added, one_mass, one_chosen)
            add_one(two_added, two_mass, two_chosen)
            return carry

        lax.fori_loop(0, lax.div(number + 1, 2), two, 0)
        if w + depth < waves:
            for copy in copies(w + depth):
                copy.start()

    scale = 1.0 / (jnp.sum(mass[:local, :], axis=1, keepdims=True) + PRIOR_MASS)
    for turn in range(ROT):
        for tile in range(width // LANES):
            line = totals[pl.ds(tile * local * SPAN + ROT - 1 - turn, local, stride=SPAN), :]
            out_ref[:, pl.ds(turn * width + tile * LANES, LANES)] = (line * scale).astype(out_ref.dtype)


def class_sum(place, buffers, weights, tables, relative, z_size, y_size, local, width, lines):
    count, size = len(buffers), buffers[0].shape[0]
    total = count * size
    wave = math.gcd(total, 128)
    depth = min(2, total // wave)
    return pl.pallas_call(
        functools.partial(sum_kernel, relative, z_size, y_size, lines, count, len(weights)),
        out_shape=jax.ShapeDtypeStruct((local, ROT * width), jnp.bfloat16),
        in_specs=[SMEM_SPEC] + [HBM_SPEC] * count + [VMEM_SPEC] * (len(weights) + 1),
        out_specs=VMEM_SPEC,
        scratch_shapes=[
            pltpu.VMEM((depth, wave, IMAGE_ROWS + META_ROWS, LANES), jnp.bfloat16),
            pltpu.VMEM((len(weights) * weights[0].shape[0], LANES), jnp.float32),
            pltpu.VMEM((2, 2 * LANES, width), jnp.bfloat16),
            pltpu.VMEM((width // LANES * local * SPAN, LANES), jnp.float32),
            pltpu.VMEM((-(-local // 8) * 8, LANES), jnp.float32),
            pltpu.VMEM((wave, LANES), jnp.int32),
            pltpu.SMEM((wave, LANES), jnp.int32),
            pltpu.SMEM((wave + 1,), jnp.int32),
            pltpu.SemaphoreType.DMA((depth, max(1, wave // size))),
            pltpu.SemaphoreType.DMA,
        ],
        compiler_params=pltpu.CompilerParams(vmem_limit_bytes=VMEM_LIMIT),
        cost_estimate=pl.CostEstimate(flops=2 * 10**10, bytes_accessed=10**7, transcendentals=0),
        name="class_sum",
    )(place, *buffers, *weights, tables)


def shards(x_size, y_size, z_size, particles, references, candidates, offsets):
    groups = lax.axis_size("cls")
    doms = lax.axis_size("dom")
    count, width = particles.shape
    local = references.shape[0]
    classes = candidates.shape[1] // 2
    block_width = width // ROT
    slots = groups * (count // 2)
    tables = jnp.asarray(trig_tables())
    place = jnp.stack([lax.axis_index("cls"), lax.axis_index("dom")]).astype(jnp.int32)

    def moves(goal):
        out = []
        for cls in range(groups):
            for dom in range(doms):
                x, core, z, y = goal(cls // 2, cls % 2, dom // y_size, dom % y_size)
                to = ((x % x_size) * 2 + core) * doms + (z % z_size) * y_size + y % y_size
                out.append((cls * doms + dom, to))
        return out

    def send(value, goal):
        return lax.ppermute(value, ("cls", "dom"), moves(goal))

    swap = functools.partial(send, goal=lambda x, c, z, y: (x, 1 - c, z, y))
    along_z = functools.partial(send, goal=lambda x, c, z, y: (x, c, z + 1, y))
    early = functools.partial(send, goal=lambda x, c, z, y: (x + 1 - c, c, z, y + c))
    late = functools.partial(send, goal=lambda x, c, z, y: (x + c, c, z, y + 1 - c))

    images = particles.reshape(count, width // LANES, LANES)
    record = jnp.concatenate([candidates, offsets], axis=1)
    mine, rest = prepare(place, record, swap(record), images, swap(images), tables, local)
    refs = references.reshape(local, ROT, block_width)
    tuned = x_size == 2 and y_size == 2
    if tuned:
        first_early, first_late = early(mine), late(mine)
        row = [mine, rest, first_early, first_late, swap(first_early), swap(first_late)]
        ring = [mine]
        for _ in range(z_size - 1):
            ring.append(along_z(ring[-1]))
        second = [first_early] + [early(part) for part in ring[1:]]
        third = [first_late] + [late(part) for part in ring[1:] + second]
        received = ring[1:] + second[1:] + third[1:]
        buffers = row + received + [swap(part) for part in received]
    else:
        row = [lax.all_gather(mine, "cls", axis=0, tiled=True)]
        buffers = [lax.all_gather(row[0], "dom", axis=0, tiled=True)]

    weights, stats, partners = score(place, row, refs, tables, slots, classes)
    if tuned:
        stats = [
            stats,
            swap(stats),
            send(stats, lambda x, c, z, y: (x + 1, c, z, y)),
            send(stats, lambda x, c, z, y: (x + 1, 1 - c, z, y)),
        ]
    else:
        stats = [lax.all_gather(stats, "cls", axis=0, tiled=False)]
    weights = normalise(tuned, place, partners, weights, stats)
    if tuned:
        weights = [
            weights if dz == dy == 0 else send(weights, lambda x, c, z, y, dz=dz, dy=dy: (x, c, z + dz, y + dy))
            for dy in range(y_size)
            for dz in range(z_size)
        ]
    else:
        weights = [lax.all_gather(weights, "dom", axis=0, tiled=True)]
    return class_sum(
        place, buffers, weights, tables, tuned, z_size, y_size, local, block_width, 2 * classes
    )


def solution(mesh):
    coords = [device.coords for device in mesh.devices.flat]
    sizes = [len({c[axis] for c in coords}) for axis in range(3)]
    in_specs = (
        P(("cls", "dom"), None),
        P("cls", None),
        P(("cls", "dom"), None),
        P(("cls", "dom"), None),
    )
    out_specs = P("cls", None)
    return jax.shard_map(
        functools.partial(shards, *sizes),
        mesh=mesh,
        in_specs=in_specs,
        out_specs=out_specs,
        check_vma=False,
    )
```

time: 174 us -> 132 us (0.76)
  waiting for transfers between devices: 75.4 us -> 31.4 us
  starting transfers between devices: 14.6 us -> 36.9 us
  blocking collectives: 14.1 us -> 0 us
  Pallas kernels: 54.5 us -> 48.8 us
    all_to_all x2 -> x0, waiting for transfers between devices: 50.3 us -> none  [the longest x1 46.1 us: shards(): lax.all_to_all(jnp.broadcast_to(stats[None], (groups * doms, *stats.shape...]
    ppermute x7 -> x42, starting transfers between devices: 6.39 us -> 36.9 us  [send(): return lax.ppermute(value, ('cls', 'dom'), moves(goal))]
    all_to_all x1 -> x0, blocking collectives: 14.1 us -> none  [shards(): lax.all_to_all(outgoing, 'cls', split_axis=0, concat_axis=0, tiled=True)]
    all_to_all x2 -> x0, starting transfers between devices: 8.17 us -> none  [the longest x1 5.58 us: shards(): lax.all_to_all(jnp.broadcast_to(weights[None], (doms, *weights.shape)), '...]
    ppermute x7 -> x42, waiting for transfers between devices: 25.1 us -> 31.4 us  [send(): return lax.ppermute(value, ('cls', 'dom'), moves(goal))]
    pallas_call x3 -> x4, Pallas kernels: 54.5 us -> 48.8 us  [the longest x1 31.5 us: class_sum(): pl.pallas_call(functools.partial(sum_kernel, relative, z_size, y_size, li...]
    broadcast_in_dim x2 -> x0, local copies, waits for them, and re-layouts: 2.89 us -> none  [the longest x1 1.48 us: shards(): jnp.broadcast_to(weights[None], (doms, *weights.shape))]
    unnamed x16 -> x88, local copies, waits for them, and re-layouts: 4.02 us -> 5.63 us
  transfers between devices with their start and end apart: 9 -> 42, of which waited for: 4 -> 11; matrix products, arithmetic and copies ran while one was open for 6% -> 7% of each run, Pallas kernels for 7% -> 10%
where the time goes in v2:
time: 132 us
  Pallas kernels  48.8 us (37%)
  starting transfers between devices  36.9 us (28%)
  waiting for transfers between devices  31.4 us (24%)
  local copies, waits for them, and re-layouts  12.7 us (10%)
  other arithmetic  1.4 us (1%)
    ppermute x42, starting transfers between devices, send(): return lax.ppermute(value, ('cls', 'dom'), moves(goal))  36.9 us
    pallas_call x1, Pallas kernels, class_sum(): pl.pallas_call(functools.partial(sum_kernel, relative, z_size, y_size, li...  31.5 us
    ppermute x42, waiting for transfers between devices, send(): return lax.ppermute(value, ('cls', 'dom'), moves(goal))  31.4 us
    pallas_call x1, Pallas kernels, score(): pl.pallas_call(functools.partial(score_kernel, count), out_shape=(jax.Sha...  11.6 us
    reshape x1, local copies, waits for them, and re-layouts, shards(): refs = references.reshape(local, ROT, block_width)  7.11 us
    unnamed x88, local copies, waits for them, and re-layouts  5.63 us
    pallas_call x1, Pallas kernels, prepare(): pl.pallas_call(functools.partial(prep_kernel, local), out_shape=(shape, s...  4.12 us
  transfers between devices with their start and end apart: 42, of which 11 were waited for; matrix products, arithmetic and copies ran while one was open for 7% of the time, Pallas kernels for 10%

profile of v2, /device:TPU:0, one launch (start us, length us, event | category | flops | bytes accessed | tf_op | source)
XLA Modules:
  0.0 131.6 jit_solution(14034333447691211067)
XLA Ops:
  0.0 1.0 copy.9
  5.5 4.1 %prepare.1 = (bf16[4,336,128]{2,1,0:T(8,128)(2,1)}, bf16[4,336,128]{2,1,0:T(8,128)(2,1)}) custom-call(s32[2]{0:T(128)} %pad_add_fusion.1.place_ref, s32[4,10]{1,0:T(4,128)} %copy-done.5, s32[4,10]{1,0:T(4,128)} %copy-done.6, bf16[4,288,128]{2,1,0:T(8,128)(2,1)} %bitcast.7, bf16[4,288,128]{2,1,0:T(8,128)(2,1)} %copy-done.1, ...), custom_call_target="tpu_custom_call" | custom-call | tf_op jit(solution)/shard_map/prepare/pallas_call | solution.py:133
  9.7 2.7 %collective-permute-start.3 = (bf16[4,336,128]{2,1,0:T(8,128)(2,1)}, bf16[4,336,128]{2,1,0:T(8,128)(2,1)S(1)}, u32[]{:S(2)}, u32[]{:S(2)}) collective-permute-start(bf16[4,336,128]{2,1,0:T(8,128)(2,1)} %get-tuple-element.10.refs_0_), channel_id=1, source_target_pairs={{0,1},{1,0},{2,3},{3,2},{4,5},{5,4},{6,7},{7,6},{8,24},{9,25},{10,... | collective-permute-start | bytes 1032200 | tf_op jit(solution)/shard_map/ppermute | solution.py:503
  12.3 1.5 %collective-permute-start.2 = (bf16[4,336,128]{2,1,0:T(8,128)(2,1)}, bf16[4,336,128]{2,1,0:T(8,128)(2,1)S(1)}, u32[]{:S(2)}, u32[]{:S(2)}) collective-permute-start(bf16[4,336,128]{2,1,0:T(8,128)(2,1)} %get-tuple-element.10.refs_0_), channel_id=1, source_target_pairs={{0,16},{1,17},{2,18},{3,19},{4,20},{5,21},{6,22},{7,23},{8,9},{9,8... | collective-permute-start | bytes 1032200 | tf_op jit(solution)/shard_map/ppermute | solution.py:503
  13.8 1.6 %collective-permute-start.6 = (bf16[4,336,128]{2,1,0:T(8,128)(2,1)}, bf16[4,336,128]{2,1,0:T(8,128)(2,1)S(1)}, u32[]{:S(2)}, u32[]{:S(2)}) collective-permute-start(bf16[4,336,128]{2,1,0:T(8,128)(2,1)} %get-tuple-element.10.refs_0_), channel_id=1, source_target_pairs={{0,2},{1,3},{2,4},{3,5},{4,6},{5,7},{6,0},{7,1},{8,10},{9,11},{10,... | collective-permute-start | bytes 1032200 | tf_op jit(solution)/shard_map/ppermute | solution.py:503
  15.4 5.2 %collective-permute-done.3.refs_3_ = bf16[4,336,128]{2,1,0:T(8,128)(2,1)S(1)} collective-permute-done((bf16[4,336,128]{2,1,0:T(8,128)(2,1)}, bf16[4,336,128]{2,1,0:T(8,128)(2,1)S(1)}, u32[]{:S(2)}, u32[]{:S(2)}) %collective-permute-start.3) | collective-permute-done | bytes 344096 | tf_op jit(solution)/shard_map/ppermute | solution.py:503
  21.6 7.1 %reshape.7.refs_6_ = bf16[50,36,1024]{2,1,0:T(8,128)(2,1)} reshape(bf16[50,36864]{1,0:T(8,128)(2,1)} %param.6) | data formatting | bytes 7372800 | tf_op jit(solution)/shard_map/reshape | solution.py:513
  28.8 2.0 %collective-permute-start.12 = (bf16[4,336,128]{2,1,0:T(8,128)(2,1)S(1)}, bf16[4,336,128]{2,1,0:T(8,128)(2,1)S(1)}, u32[]{:S(2)}, u32[]{:S(2)}) collective-permute-start(bf16[4,336,128]{2,1,0:T(8,128)(2,1)S(1)} %collective-permute-done.6.refs_6_), channel_id=1, source_target_pairs={{0,1},{1,0},{2,3},{3,2},{4,5},{5,4},{6,7},{7,6},{8,24},{9,25},{10,... | collective-permute-start | bytes 1032200 | tf_op jit(solution)/shard_map/ppermute | solution.py:503
  31.7 11.6 %score.1 = (f32[8,8,128]{2,1,0:T(8,128)}, f32[16,128]{1,0:T(8,128)}, s32[8,3]{1,0:T(8,128)}) custom-call(s32[2]{0:T(128)} %pad_add_fusion.1.place_ref, bf16[4,336,128]{2,1,0:T(8,128)(2,1)} %get-tuple-element.10.refs_0_, bf16[4,336,128]{2,1,0:T(8,128)(2,1)} %get-tuple-element.11.refs_1_, bf16[4,336,128]{2,1,0:T(8,128)(2,1)} %copy-done.8, ...), custom_call_target="tpu_custom_call" | custom-call | flops 10000000000 | bytes 10000000 | tf_op jit(solution)/shard_map/score/pallas_call | solution.py:271
  43.4 1.6 %collective-permute-start.33 = (f32[16,128]{1,0:T(8,128)}, f32[16,128]{1,0:T(8,128)S(1)}, u32[]{:S(2)}, u32[]{:S(2)}) collective-permute-start(f32[16,128]{1,0:T(8,128)} %get-tuple-element.14.refs_0_), channel_id=1, source_target_pairs={{0,16},{1,17},{2,18},{3,19},{4,20},{5,21},{6,22},{7,23},{8,24},{9,... | collective-permute-start | bytes 24584 | tf_op jit(solution)/shard_map/ppermute | solution.py:503
  45.3 1.4 %collective-permute-done.34.refs_3_ = f32[16,128]{1,0:T(8,128)S(1)} collective-permute-done((f32[16,128]{1,0:T(8,128)}, f32[16,128]{1,0:T(8,128)S(1)}, u32[]{:S(2)}, u32[]{:S(2)}) %collective-permute-start.34) | collective-permute-done | bytes 8224 | tf_op jit(solution)/shard_map/ppermute | solution.py:503
  46.7 1.5 %collective-permute-start.9 = (bf16[4,336,128]{2,1,0:T(8,128)(2,1)S(1)}, bf16[4,336,128]{2,1,0:T(8,128)(2,1)S(1)}, u32[]{:S(2)}, u32[]{:S(2)}) collective-permute-start(bf16[4,336,128]{2,1,0:T(8,128)(2,1)S(1)} %collective-permute-done.6.refs_6_), channel_id=1, source_target_pairs={{0,16},{1,17},{2,18},{3,19},{4,20},{5,21},{6,22},{7,23},{8,9},{9,8... | collective-permute-start | bytes 1032200 | tf_op jit(solution)/shard_map/ppermute | solution.py:503
  48.2 1.6 %collective-permute-start.7 = (bf16[4,336,128]{2,1,0:T(8,128)(2,1)S(1)}, bf16[4,336,128]{2,1,0:T(8,128)(2,1)S(1)}, u32[]{:S(2)}, u32[]{:S(2)}) collective-permute-start(bf16[4,336,128]{2,1,0:T(8,128)(2,1)S(1)} %collective-permute-done.6.refs_6_), channel_id=1, source_target_pairs={{0,2},{1,3},{2,4},{3,5},{4,6},{5,7},{6,0},{7,1},{8,10},{9,11},{10,... | collective-permute-start | bytes 1032200 | tf_op jit(solution)/shard_map/ppermute | solution.py:503
  50.6 1.5 %normalise.1.refs_32_ = bf16[64,128]{1,0:T(8,128)(2,1)} custom-call(s32[2]{0:T(128)} %pad_add_fusion.1.place_ref, s32[8,3]{1,0:T(8,128)} %get-tuple-element.12.partner_ref, f32[8,8,128]{2,1,0:T(8,128)} %get-tuple-element.13.weight_ref, f32[16,128]{1,0:T(8,128)} %get-tuple-element.14.refs_0_, f32[16,128]{1,0:T(8,128)} %copy-done.4, f32[16,128]{1,0:T(8,128)} %copy-done.3, ...), custom_call_target="tpu_custom_call" | custom-call | tf_op jit(solution)/shard_map/normalise/pallas_call | solution.py:320
  52.2 3.0 %collective-permute-start.41 = (bf16[64,128]{1,0:T(8,128)(2,1)}, bf16[64,128]{1,0:T(8,128)(2,1)S(1)}, u32[]{:S(2)}, u32[]{:S(2)}) collective-permute-start(bf16[64,128]{1,0:T(8,128)(2,1)} %normalise.1.refs_32_), channel_id=1, source_target_pairs={{0,7},{1,6},{2,1},{3,0},{4,3},{5,2},{6,5},{7,4},{8,15},{9,14},{10,... | collective-permute-start | bytes 49160 | tf_op jit(solution)/shard_map/ppermute | solution.py:503
  55.2 0.9 collective-permute-start.40
  56.1 2.4 %collective-permute-start.39 = (bf16[64,128]{1,0:T(8,128)(2,1)}, bf16[64,128]{1,0:T(8,128)(2,1)S(1)}, u32[]{:S(2)}, u32[]{:S(2)}) collective-permute-start(bf16[64,128]{1,0:T(8,128)(2,1)} %normalise.1.refs_32_), channel_id=1, source_target_pairs={{0,3},{1,2},{2,5},{3,4},{4,7},{5,6},{6,1},{7,0},{8,11},{9,10},{10,... | collective-permute-start | bytes 49160 | tf_op jit(solution)/shard_map/ppermute | solution.py:503
  58.5 2.0 %collective-permute-done.7.refs_7_ = bf16[4,336,128]{2,1,0:T(8,128)(2,1)S(1)} collective-permute-done((bf16[4,336,128]{2,1,0:T(8,128)(2,1)S(1)}, bf16[4,336,128]{2,1,0:T(8,128)(2,1)S(1)}, u32[]{:S(2)}, u32[]{:S(2)}) %collective-permute-start.7) | collective-permute-done | bytes 344096 | tf_op jit(solution)/shard_map/ppermute | solution.py:503
  60.9 2.0 %collective-permute-start.37 = (bf16[64,128]{1,0:T(8,128)(2,1)}, bf16[64,128]{1,0:T(8,128)(2,1)S(1)}, u32[]{:S(2)}, u32[]{:S(2)}) collective-permute-start(bf16[64,128]{1,0:T(8,128)(2,1)} %normalise.1.refs_32_), channel_id=1, source_target_pairs={{0,6},{1,7},{2,0},{3,1},{4,2},{5,3},{6,4},{7,5},{8,14},{9,15},{10,... | collective-permute-start | bytes 49160 | tf_op jit(solution)/shard_map/ppermute | solution.py:503
  63.0 1.8 %collective-permute-start.35 = (bf16[64,128]{1,0:T(8,128)(2,1)}, bf16[64,128]{1,0:T(8,128)(2,1)S(1)}, u32[]{:S(2)}, u32[]{:S(2)}) collective-permute-start(bf16[64,128]{1,0:T(8,128)(2,1)} %normalise.1.refs_32_), channel_id=1, source_target_pairs={{0,2},{1,3},{2,4},{3,5},{4,6},{5,7},{6,0},{7,1},{8,10},{9,11},{10,... | collective-permute-start | bytes 49160 | tf_op jit(solution)/shard_map/ppermute | solution.py:503
  65.3 1.1 collective-permute-start.16
  66.4 1.4 %collective-permute-done.36.refs_34_ = bf16[64,128]{1,0:T(8,128)(2,1)S(1)} collective-permute-done((bf16[64,128]{1,0:T(8,128)(2,1)}, bf16[64,128]{1,0:T(8,128)(2,1)S(1)}, u32[]{:S(2)}, u32[]{:S(2)}) %collective-permute-start.36) | collective-permute-done | bytes 16416 | tf_op jit(solution)/shard_map/ppermute | solution.py:503
  67.8 1.0 collective-permute-done.35.refs_33_
  68.8 1.1 collective-permute-start.13
  69.9 1.0 collective-permute-start.10
  71.0 2.5 %collective-permute-done.16.refs_16_ = bf16[4,336,128]{2,1,0:T(8,128)(2,1)S(1)} collective-permute-done((bf16[4,336,128]{2,1,0:T(8,128)(2,1)S(1)}, bf16[4,336,128]{2,1,0:T(8,128)(2,1)S(1)}, u32[]{:S(2)}, u32[]{:S(2)}) %collective-permute-start.16) | collective-permute-done | bytes 344096 | tf_op jit(solution)/shard_map/ppermute | solution.py:503
  74.0 6.1 %collective-permute-done.8.refs_8_ = bf16[4,336,128]{2,1,0:T(8,128)(2,1)S(1)} collective-permute-done((bf16[4,336,128]{2,1,0:T(8,128)(2,1)S(1)}, bf16[4,336,128]{2,1,0:T(8,128)(2,1)S(1)}, u32[]{:S(2)}, u32[]{:S(2)}) %collective-permute-start.8) | collective-permute-done | bytes 344096 | tf_op jit(solution)/shard_map/ppermute | solution.py:503
  81.2 1.5 %collective-permute-start.17 = (bf16[4,336,128]{2,1,0:T(8,128)(2,1)S(1)}, bf16[4,336,128]{2,1,0:T(8,128)(2,1)S(1)}, u32[]{:S(2)}, u32[]{:S(2)}) collective-permute-start(bf16[4,336,128]{2,1,0:T(8,128)(2,1)S(1)} %collective-permute-done.10.refs_10_), channel_id=1, source_target_pairs={{0,1},{1,0},{2,3},{3,2},{4,5},{5,4},{6,7},{7,6},{8,24},{9,25},{10,... | collective-permute-start | bytes 1032200 | tf_op jit(solution)/shard_map/ppermute | solution.py:503
  83.2 7.6 %collective-permute-done.11.refs_11_ = bf16[4,336,128]{2,1,0:T(8,128)(2,1)S(1)} collective-permute-done((bf16[4,336,128]{2,1,0:T(8,128)(2,1)S(1)}, bf16[4,336,128]{2,1,0:T(8,128)(2,1)S(1)}, u32[]{:S(2)}, u32[]{:S(2)}) %collective-permute-start.11) | collective-permute-done | bytes 344096 | tf_op jit(solution)/shard_map/ppermute | solution.py:503
  92.4 2.5 %collective-permute-start.27 = (bf16[4,336,128]{2,1,0:T(8,128)(2,1)S(1)}, bf16[4,336,128]{2,1,0:T(8,128)(2,1)S(1)}, u32[]{:S(2)}, u32[]{:S(2)}) collective-permute-start(bf16[4,336,128]{2,1,0:T(8,128)(2,1)S(1)} %collective-permute-done.14.refs_14_), channel_id=1, source_target_pairs={{0,8},{1,9},{2,10},{3,11},{4,12},{5,13},{6,14},{7,15},{8,0},{9,1},... | collective-permute-start | bytes 1032200 | tf_op jit(solution)/shard_map/ppermute | solution.py:503
  94.8 3.2 %collective-permute-done.18.refs_18_ = bf16[4,336,128]{2,1,0:T(8,128)(2,1)S(1)} collective-permute-done((bf16[4,336,128]{2,1,0:T(8,128)(2,1)S(1)}, bf16[4,336,128]{2,1,0:T(8,128)(2,1)S(1)}, u32[]{:S(2)}, u32[]{:S(2)}) %collective-permute-start.18) | collective-permute-done | bytes 344096 | tf_op jit(solution)/shard_map/ppermute | solution.py:503
  100.1 31.5 %class_sum.1 = bf16[50,36864]{1,0:T(8,128)(2,1)} custom-call(s32[2]{0:T(128)} %pad_add_fusion.1.place_ref, bf16[4,336,128]{2,1,0:T(8,128)(2,1)} %get-tuple-element.10.refs_0_, bf16[4,336,128]{2,1,0:T(8,128)(2,1)} %get-tuple-element.11.refs_1_, bf16[4,336,128]{2,1,0:T(8,128)(2,1)} %copy-done.8, bf16[4,336,128]{2,1,0:T(8,128)(2,1)} %copy-done.7, ...), custom_call_target="tpu_custom_call" | custom-call | flops 20000000000 | bytes 10000000 | tf_op jit(solution)/shard_map/class_sum/pallas_call | solution.py:459
  (147 shorter events, 14.0 us)
Async XLA Ops:
  9.7 10.9 %collective-permute-start.3 = (bf16[4,336,128]{2,1,0:T(8,128)(2,1)}, bf16[4,336,128]{2,1,0:T(8,128)(2,1)S(1)}, u32[]{:S(2)}, u32[]{:S(2)}) collective-permute-start(bf16[4,336,128]{2,1,0:T(8,128)(2,1)} %get-tuple-element.10.refs_0_), channel_id=1, source_target_pairs={{0,1},{1,0},{2,3},{3,2},{4,5},{5,4},{6,7},{7,6},{8,24},{9,25},{10,... | collective-permute-start | bytes 1032200 | tf_op jit(solution)/shard_map/ppermute | solution.py:503
  12.3 8.7 %collective-permute-start.2 = (bf16[4,336,128]{2,1,0:T(8,128)(2,1)}, bf16[4,336,128]{2,1,0:T(8,128)(2,1)S(1)}, u32[]{:S(2)}, u32[]{:S(2)}) collective-permute-start(bf16[4,336,128]{2,1,0:T(8,128)(2,1)} %get-tuple-element.10.refs_0_), channel_id=1, source_target_pairs={{0,16},{1,17},{2,18},{3,19},{4,20},{5,21},{6,22},{7,23},{8,9},{9,8... | collective-permute-start | bytes 1032200 | tf_op jit(solution)/shard_map/ppermute | solution.py:503
  13.8 14.9 %collective-permute-start.6 = (bf16[4,336,128]{2,1,0:T(8,128)(2,1)}, bf16[4,336,128]{2,1,0:T(8,128)(2,1)S(1)}, u32[]{:S(2)}, u32[]{:S(2)}) collective-permute-start(bf16[4,336,128]{2,1,0:T(8,128)(2,1)} %get-tuple-element.10.refs_0_), channel_id=1, source_target_pairs={{0,2},{1,3},{2,4},{3,5},{4,6},{5,7},{6,0},{7,1},{8,10},{9,11},{10,... | collective-permute-start | bytes 1032200 | tf_op jit(solution)/shard_map/ppermute | solution.py:503
  20.6 10.3 %collective-permute-start.5 = (bf16[4,336,128]{2,1,0:T(8,128)(2,1)S(1)}, bf16[4,336,128]{2,1,0:T(8,128)(2,1)S(1)}, u32[]{:S(2)}, u32[]{:S(2)}) collective-permute-start(bf16[4,336,128]{2,1,0:T(8,128)(2,1)S(1)} %collective-permute-done.3.refs_3_), channel_id=1, source_target_pairs={{0,8},{1,9},{2,10},{3,11},{4,12},{5,13},{6,14},{7,15},{8,0},{9,1},... | collective-permute-start | bytes 1032200 | tf_op jit(solution)/shard_map/ppermute | solution.py:503
  21.1 9.8 %collective-permute-start.4 = (bf16[4,336,128]{2,1,0:T(8,128)(2,1)S(1)}, bf16[4,336,128]{2,1,0:T(8,128)(2,1)S(1)}, u32[]{:S(2)}, u32[]{:S(2)}) collective-permute-start(bf16[4,336,128]{2,1,0:T(8,128)(2,1)S(1)} %collective-permute-done.2.refs_2_), channel_id=1, source_target_pairs={{0,8},{1,9},{2,10},{3,11},{4,12},{5,13},{6,14},{7,15},{8,0},{9,1},... | collective-permute-start | bytes 1032200 | tf_op jit(solution)/shard_map/ppermute | solution.py:503
  28.7 23.5 %collective-permute-start.19 = (bf16[4,336,128]{2,1,0:T(8,128)(2,1)S(1)}, bf16[4,336,128]{2,1,0:T(8,128)(2,1)S(1)}, u32[]{:S(2)}, u32[]{:S(2)}) collective-permute-start(bf16[4,336,128]{2,1,0:T(8,128)(2,1)S(1)} %collective-permute-done.6.refs_6_), channel_id=1, source_target_pairs={{0,8},{1,9},{2,10},{3,11},{4,12},{5,13},{6,14},{7,15},{8,0},{9,1},... | collective-permute-start | bytes 1032200 | tf_op jit(solution)/shard_map/ppermute | solution.py:503
  28.8 26.3 %collective-permute-start.12 = (bf16[4,336,128]{2,1,0:T(8,128)(2,1)S(1)}, bf16[4,336,128]{2,1,0:T(8,128)(2,1)S(1)}, u32[]{:S(2)}, u32[]{:S(2)}) collective-permute-start(bf16[4,336,128]{2,1,0:T(8,128)(2,1)S(1)} %collective-permute-done.6.refs_6_), channel_id=1, source_target_pairs={{0,1},{1,0},{2,3},{3,2},{4,5},{5,4},{6,7},{7,6},{8,24},{9,25},{10,... | collective-permute-start | bytes 1032200 | tf_op jit(solution)/shard_map/ppermute | solution.py:503
  46.7 9.4 %collective-permute-start.9 = (bf16[4,336,128]{2,1,0:T(8,128)(2,1)S(1)}, bf16[4,336,128]{2,1,0:T(8,128)(2,1)S(1)}, u32[]{:S(2)}, u32[]{:S(2)}) collective-permute-start(bf16[4,336,128]{2,1,0:T(8,128)(2,1)S(1)} %collective-permute-done.6.refs_6_), channel_id=1, source_target_pairs={{0,16},{1,17},{2,18},{3,19},{4,20},{5,21},{6,22},{7,23},{8,9},{9,8... | collective-permute-start | bytes 1032200 | tf_op jit(solution)/shard_map/ppermute | solution.py:503
  48.2 12.2 %collective-permute-start.7 = (bf16[4,336,128]{2,1,0:T(8,128)(2,1)S(1)}, bf16[4,336,128]{2,1,0:T(8,128)(2,1)S(1)}, u32[]{:S(2)}, u32[]{:S(2)}) collective-permute-start(bf16[4,336,128]{2,1,0:T(8,128)(2,1)S(1)} %collective-permute-done.6.refs_6_), channel_id=1, source_target_pairs={{0,2},{1,3},{2,4},{3,5},{4,6},{5,7},{6,0},{7,1},{8,10},{9,11},{10,... | collective-permute-start | bytes 1032200 | tf_op jit(solution)/shard_map/ppermute | solution.py:503
  49.9 11.0 %collective-permute-start.15 = (bf16[4,336,128]{2,1,0:T(8,128)(2,1)}, bf16[4,336,128]{2,1,0:T(8,128)(2,1)S(1)}, u32[]{:S(2)}, u32[]{:S(2)}) collective-permute-start(bf16[4,336,128]{2,1,0:T(8,128)(2,1)} %copy-done.8), channel_id=1, source_target_pairs={{0,1},{1,0},{2,3},{3,2},{4,5},{5,4},{6,7},{7,6},{8,24},{9,25},{10,... | collective-permute-start | bytes 1032200 | tf_op jit(solution)/shard_map/ppermute | solution.py:503
  52.2 10.8 %collective-permute-start.41 = (bf16[64,128]{1,0:T(8,128)(2,1)}, bf16[64,128]{1,0:T(8,128)(2,1)S(1)}, u32[]{:S(2)}, u32[]{:S(2)}) collective-permute-start(bf16[64,128]{1,0:T(8,128)(2,1)} %normalise.1.refs_32_), channel_id=1, source_target_pairs={{0,7},{1,6},{2,1},{3,0},{4,3},{5,2},{6,5},{7,4},{8,15},{9,14},{10,... | collective-permute-start | bytes 49160 | tf_op jit(solution)/shard_map/ppermute | solution.py:503
  55.2 7.8 %collective-permute-start.40 = (bf16[64,128]{1,0:T(8,128)(2,1)}, bf16[64,128]{1,0:T(8,128)(2,1)S(1)}, u32[]{:S(2)}, u32[]{:S(2)}) collective-permute-start(bf16[64,128]{1,0:T(8,128)(2,1)} %normalise.1.refs_32_), channel_id=1, source_target_pairs={{0,5},{1,4},{2,7},{3,6},{4,1},{5,0},{6,3},{7,2},{8,13},{9,12},{10,... | collective-permute-start | bytes 49160 | tf_op jit(solution)/shard_map/ppermute | solution.py:503
  56.1 8.7 %collective-permute-start.39 = (bf16[64,128]{1,0:T(8,128)(2,1)}, bf16[64,128]{1,0:T(8,128)(2,1)S(1)}, u32[]{:S(2)}, u32[]{:S(2)}) collective-permute-start(bf16[64,128]{1,0:T(8,128)(2,1)} %normalise.1.refs_32_), channel_id=1, source_target_pairs={{0,3},{1,2},{2,5},{3,4},{4,7},{5,6},{6,1},{7,0},{8,11},{9,10},{10,... | collective-permute-start | bytes 49160 | tf_op jit(solution)/shard_map/ppermute | solution.py:503
  63.0 5.8 %collective-permute-start.35 = (bf16[64,128]{1,0:T(8,128)(2,1)}, bf16[64,128]{1,0:T(8,128)(2,1)S(1)}, u32[]{:S(2)}, u32[]{:S(2)}) collective-permute-start(bf16[64,128]{1,0:T(8,128)(2,1)} %normalise.1.refs_32_), channel_id=1, source_target_pairs={{0,2},{1,3},{2,4},{3,5},{4,6},{5,7},{6,0},{7,1},{8,10},{9,11},{10,... | collective-permute-start | bytes 49160 | tf_op jit(solution)/shard_map/ppermute | solution.py:503
  64.8 5.1 %collective-permute-start.22 = (bf16[4,336,128]{2,1,0:T(8,128)(2,1)S(1)}, bf16[4,336,128]{2,1,0:T(8,128)(2,1)S(1)}, u32[]{:S(2)}, u32[]{:S(2)}) collective-permute-start(bf16[4,336,128]{2,1,0:T(8,128)(2,1)S(1)} %collective-permute-done.9.refs_9_), channel_id=1, source_target_pairs={{0,8},{1,9},{2,10},{3,11},{4,12},{5,13},{6,14},{7,15},{8,0},{9,1},... | collective-permute-start | bytes 1032200 | tf_op jit(solution)/shard_map/ppermute | solution.py:503
  65.3 8.1 %collective-permute-start.16 = (bf16[4,336,128]{2,1,0:T(8,128)(2,1)S(1)}, bf16[4,336,128]{2,1,0:T(8,128)(2,1)S(1)}, u32[]{:S(2)}, u32[]{:S(2)}) collective-permute-start(bf16[4,336,128]{2,1,0:T(8,128)(2,1)S(1)} %collective-permute-done.9.refs_9_), channel_id=1, source_target_pairs={{0,1},{1,0},{2,3},{3,2},{4,5},{5,4},{6,7},{7,6},{8,24},{9,25},{10,... | collective-permute-start | bytes 1032200 | tf_op jit(solution)/shard_map/ppermute | solution.py:503
  67.8 5.7 %collective-permute-start.20 = (bf16[4,336,128]{2,1,0:T(8,128)(2,1)S(1)}, bf16[4,336,128]{2,1,0:T(8,128)(2,1)S(1)}, u32[]{:S(2)}, u32[]{:S(2)}) collective-permute-start(bf16[4,336,128]{2,1,0:T(8,128)(2,1)S(1)} %collective-permute-done.7.refs_7_), channel_id=1, source_target_pairs={{0,8},{1,9},{2,10},{3,11},{4,12},{5,13},{6,14},{7,15},{8,0},{9,1},... | collective-permute-start | bytes 1032200 | tf_op jit(solution)/shard_map/ppermute | solution.py:503
  68.8 11.3 %collective-permute-start.8 = (bf16[4,336,128]{2,1,0:T(8,128)(2,1)S(1)}, bf16[4,336,128]{2,1,0:T(8,128)(2,1)S(1)}, u32[]{:S(2)}, u32[]{:S(2)}) collective-permute-start(bf16[4,336,128]{2,1,0:T(8,128)(2,1)S(1)} %collective-permute-done.7.refs_7_), channel_id=1, source_target_pairs={{0,2},{1,3},{2,4},{3,5},{4,6},{5,7},{6,0},{7,1},{8,10},{9,11},{10,... | collective-permute-start | bytes 1032200 | tf_op jit(solution)/shard_map/ppermute | solution.py:503
  68.8 11.8 %collective-permute-start.13 = (bf16[4,336,128]{2,1,0:T(8,128)(2,1)S(1)}, bf16[4,336,128]{2,1,0:T(8,128)(2,1)S(1)}, u32[]{:S(2)}, u32[]{:S(2)}) collective-permute-start(bf16[4,336,128]{2,1,0:T(8,128)(2,1)S(1)} %collective-permute-done.7.refs_7_), channel_id=1, source_target_pairs={{0,1},{1,0},{2,3},{3,2},{4,5},{5,4},{6,7},{7,6},{8,24},{9,25},{10,... | collective-permute-start | bytes 1032200 | tf_op jit(solution)/shard_map/ppermute | solution.py:503
  69.9 10.7 %collective-permute-start.10 = (bf16[4,336,128]{2,1,0:T(8,128)(2,1)S(1)}, bf16[4,336,128]{2,1,0:T(8,128)(2,1)S(1)}, u32[]{:S(2)}, u32[]{:S(2)}) collective-permute-start(bf16[4,336,128]{2,1,0:T(8,128)(2,1)S(1)} %collective-permute-done.7.refs_7_), channel_id=1, source_target_pairs={{0,16},{1,17},{2,18},{3,19},{4,20},{5,21},{6,22},{7,23},{8,9},{9,8... | collective-permute-start | bytes 1032200 | tf_op jit(solution)/shard_map/ppermute | solution.py:503
  73.4 7.7 %collective-permute-start.28 = (bf16[4,336,128]{2,1,0:T(8,128)(2,1)S(1)}, bf16[4,336,128]{2,1,0:T(8,128)(2,1)S(1)}, u32[]{:S(2)}, u32[]{:S(2)}) collective-permute-start(bf16[4,336,128]{2,1,0:T(8,128)(2,1)S(1)} %collective-permute-done.15.refs_15_), channel_id=1, source_target_pairs={{0,8},{1,9},{2,10},{3,11},{4,12},{5,13},{6,14},{7,15},{8,0},{9,1},... | collective-permute-start | bytes 1032200 | tf_op jit(solution)/shard_map/ppermute | solution.py:503
  73.5 9.2 %collective-permute-start.29 = (bf16[4,336,128]{2,1,0:T(8,128)(2,1)S(1)}, bf16[4,336,128]{2,1,0:T(8,128)(2,1)S(1)}, u32[]{:S(2)}, u32[]{:S(2)}) collective-permute-start(bf16[4,336,128]{2,1,0:T(8,128)(2,1)S(1)} %collective-permute-done.16.refs_16_), channel_id=1, source_target_pairs={{0,8},{1,9},{2,10},{3,11},{4,12},{5,13},{6,14},{7,15},{8,0},{9,1},... | collective-permute-start | bytes 1032200 | tf_op jit(solution)/shard_map/ppermute | solution.py:503
  80.1 10.7 %collective-permute-start.11 = (bf16[4,336,128]{2,1,0:T(8,128)(2,1)S(1)}, bf16[4,336,128]{2,1,0:T(8,128)(2,1)S(1)}, u32[]{:S(2)}, u32[]{:S(2)}) collective-permute-start(bf16[4,336,128]{2,1,0:T(8,128)(2,1)S(1)} %collective-permute-done.8.refs_8_), channel_id=1, source_target_pairs={{0,16},{1,17},{2,18},{3,19},{4,20},{5,21},{6,22},{7,23},{8,9},{9,8... | collective-permute-start | bytes 1032200 | tf_op jit(solution)/shard_map/ppermute | solution.py:503
  80.6 11.1 %collective-permute-start.26 = (bf16[4,336,128]{2,1,0:T(8,128)(2,1)S(1)}, bf16[4,336,128]{2,1,0:T(8,128)(2,1)S(1)}, u32[]{:S(2)}, u32[]{:S(2)}) collective-permute-start(bf16[4,336,128]{2,1,0:T(8,128)(2,1)S(1)} %collective-permute-done.13.refs_13_), channel_id=1, source_target_pairs={{0,8},{1,9},{2,10},{3,11},{4,12},{5,13},{6,14},{7,15},{8,0},{9,1},... | collective-permute-start | bytes 1032200 | tf_op jit(solution)/shard_map/ppermute | solution.py:503
  80.7 11.1 %collective-permute-start.23 = (bf16[4,336,128]{2,1,0:T(8,128)(2,1)S(1)}, bf16[4,336,128]{2,1,0:T(8,128)(2,1)S(1)}, u32[]{:S(2)}, u32[]{:S(2)}) collective-permute-start(bf16[4,336,128]{2,1,0:T(8,128)(2,1)S(1)} %collective-permute-done.10.refs_10_), channel_id=1, source_target_pairs={{0,8},{1,9},{2,10},{3,11},{4,12},{5,13},{6,14},{7,15},{8,0},{9,1},... | collective-permute-start | bytes 1032200 | tf_op jit(solution)/shard_map/ppermute | solution.py:503
  81.2 11.1 %collective-permute-start.17 = (bf16[4,336,128]{2,1,0:T(8,128)(2,1)S(1)}, bf16[4,336,128]{2,1,0:T(8,128)(2,1)S(1)}, u32[]{:S(2)}, u32[]{:S(2)}) collective-permute-start(bf16[4,336,128]{2,1,0:T(8,128)(2,1)S(1)} %collective-permute-done.10.refs_10_), channel_id=1, source_target_pairs={{0,1},{1,0},{2,3},{3,2},{4,5},{5,4},{6,7},{7,6},{8,24},{9,25},{10,... | collective-permute-start | bytes 1032200 | tf_op jit(solution)/shard_map/ppermute | solution.py:503
  82.7 9.7 %collective-permute-start.14 = (bf16[4,336,128]{2,1,0:T(8,128)(2,1)S(1)}, bf16[4,336,128]{2,1,0:T(8,128)(2,1)S(1)}, u32[]{:S(2)}, u32[]{:S(2)}) collective-permute-start(bf16[4,336,128]{2,1,0:T(8,128)(2,1)S(1)} %collective-permute-done.8.refs_8_), channel_id=1, source_target_pairs={{0,1},{1,0},{2,3},{3,2},{4,5},{5,4},{6,7},{7,6},{8,24},{9,25},{10,... | collective-permute-start | bytes 1032200 | tf_op jit(solution)/shard_map/ppermute | solution.py:503
  90.8 7.2 %collective-permute-start.18 = (bf16[4,336,128]{2,1,0:T(8,128)(2,1)S(1)}, bf16[4,336,128]{2,1,0:T(8,128)(2,1)S(1)}, u32[]{:S(2)}, u32[]{:S(2)}) collective-permute-start(bf16[4,336,128]{2,1,0:T(8,128)(2,1)S(1)} %collective-permute-done.11.refs_11_), channel_id=1, source_target_pairs={{0,1},{1,0},{2,3},{3,2},{4,5},{5,4},{6,7},{7,6},{8,24},{9,25},{10,... | collective-permute-start | bytes 1032200 | tf_op jit(solution)/shard_map/ppermute | solution.py:503
  91.7 6.5 %collective-permute-start.21 = (bf16[4,336,128]{2,1,0:T(8,128)(2,1)S(1)}, bf16[4,336,128]{2,1,0:T(8,128)(2,1)S(1)}, u32[]{:S(2)}, u32[]{:S(2)}) collective-permute-start(bf16[4,336,128]{2,1,0:T(8,128)(2,1)S(1)} %collective-permute-done.8.refs_8_), channel_id=1, source_target_pairs={{0,8},{1,9},{2,10},{3,11},{4,12},{5,13},{6,14},{7,15},{8,0},{9,1},... | collective-permute-start | bytes 1032200 | tf_op jit(solution)/shard_map/ppermute | solution.py:503
  91.8 6.5 %collective-permute-start.24 = (bf16[4,336,128]{2,1,0:T(8,128)(2,1)S(1)}, bf16[4,336,128]{2,1,0:T(8,128)(2,1)S(1)}, u32[]{:S(2)}, u32[]{:S(2)}) collective-permute-start(bf16[4,336,128]{2,1,0:T(8,128)(2,1)S(1)} %collective-permute-done.11.refs_11_), channel_id=1, source_target_pairs={{0,8},{1,9},{2,10},{3,11},{4,12},{5,13},{6,14},{7,15},{8,0},{9,1},... | collective-permute-start | bytes 1032200 | tf_op jit(solution)/shard_map/ppermute | solution.py:503
  92.2 6.0 %collective-permute-start.30 = (bf16[4,336,128]{2,1,0:T(8,128)(2,1)S(1)}, bf16[4,336,128]{2,1,0:T(8,128)(2,1)S(1)}, u32[]{:S(2)}, u32[]{:S(2)}) collective-permute-start(bf16[4,336,128]{2,1,0:T(8,128)(2,1)S(1)} %collective-permute-done.17.refs_17_), channel_id=1, source_target_pairs={{0,8},{1,9},{2,10},{3,11},{4,12},{5,13},{6,14},{7,15},{8,0},{9,1},... | collective-permute-start | bytes 1032200 | tf_op jit(solution)/shard_map/ppermute | solution.py:503
  92.4 5.9 %collective-permute-start.27 = (bf16[4,336,128]{2,1,0:T(8,128)(2,1)S(1)}, bf16[4,336,128]{2,1,0:T(8,128)(2,1)S(1)}, u32[]{:S(2)}, u32[]{:S(2)}) collective-permute-start(bf16[4,336,128]{2,1,0:T(8,128)(2,1)S(1)} %collective-permute-done.14.refs_14_), channel_id=1, source_target_pairs={{0,8},{1,9},{2,10},{3,11},{4,12},{5,13},{6,14},{7,15},{8,0},{9,1},... | collective-permute-start | bytes 1032200 | tf_op jit(solution)/shard_map/ppermute | solution.py:503
  (53 other events, 789.4 us)

commit v3 on v2

--- a/solution.py
+++ b/solution.py
@@ -168,7 +168,7 @@
     re = values[2 * step * SPAN : (2 * step + 1) * SPAN]
     im = values[(2 * step + 1) * SPAN : (2 * step + 2) * SPAN]
     at = pl.ds(step * SPAN, SPAN)
-    return re, im, [table_ref[k, 1, at, :] for k in range(4)]
+    return re, im, [table_ref[k, at, :] for k in range(4)]
 
 
 def store_moved(moved, step, part, blocks):
@@ -178,12 +178,12 @@
     moved[LANES : LANES + 2 * SPAN, at] = jnp.concatenate(blocks[3:], axis=0).astype(jnp.bfloat16)
 
 
-def score_kernel(count, place_ref, *refs):
+def score_kernel(count, waits, place_ref, *refs):
     image_refs = refs[:count]
     (
         refs_ref, table_ref, weight_ref, stat_ref, partner_ref,
         moved, picked, sums, meta_vmem, meta, sem,
-    ) = refs[count:]
+    ) = refs[count + waits :]
     block = image_refs[0].shape[0]
     slots = weight_ref.shape[0]
     classes = picked.shape[0] // 48
@@ -265,17 +265,17 @@
         lax.fori_loop(0, block, body, 0)
 
 
-def score(place, buffers, refs, tables, slots, classes):
+def score(place, buffers, refs, tables, slots, classes, after):
     count, block = len(buffers), buffers[0].shape[0]
     width = refs.shape[2]
     return pl.pallas_call(
-        functools.partial(score_kernel, count),
+        functools.partial(score_kernel, count, len(after)),
         out_shape=(
             jax.ShapeDtypeStruct((slots, 2 * classes, LANES), jnp.float32),
             jax.ShapeDtypeStruct((2 * slots, LANES), jnp.float32),
             jax.ShapeDtypeStruct((slots, 3), jnp.int32),
         ),
-        in_specs=[SMEM_SPEC] + [VMEM_SPEC] * (count + 2),
+        in_specs=[SMEM_SPEC] + [VMEM_SPEC] * count + [HBM_SPEC] * len(after) + [VMEM_SPEC] * 2,
         out_specs=(VMEM_SPEC, VMEM_SPEC, SMEM_SPEC),
         scratch_shapes=[
             pltpu.VMEM((2 * LANES, width), jnp.bfloat16),
@@ -288,7 +288,7 @@
         compiler_params=pltpu.CompilerParams(vmem_limit_bytes=VMEM_LIMIT),
         cost_estimate=pl.CostEstimate(flops=10**10, bytes_accessed=10**7, transcendentals=0),
         name="score",
-    )(place, *buffers, refs, tables)
+    )(place, *buffers, *after, refs, tables)
 
 
 def weight_kernel(flip, place_ref, partner_ref, weight_ref, *refs):
@@ -326,43 +326,50 @@
     )(place, partners, weights, *stats)
 
 
-def sum_kernel(relative, z_size, y_size, lines, count, n_weights, place_ref, *refs):
-    image_refs = refs[:count]
-    weight_refs = refs[count : count + n_weights]
-    (
-        table_ref, out_ref, images, weights, moved, totals, mass, meta_vmem, meta, active, image_sem, meta_sem,
-    ) = refs[count + n_weights :]
-    local = out_ref.shape[0]
-    width = moved.shape[2]
+def sum_kernel(weight_rows, relative, z_size, y_size, lines, local, width, count, n_weights, first, last, place_ref, *refs):
+    refs = list(refs)
+    image_refs = [refs.pop(0) for _ in range(count)]
+    weight_refs = [refs.pop(0) for _ in range(n_weights)]
+    table_ref = refs.pop(0)
+    given = None if first else [refs.pop(0), refs.pop(0)]
+    out_ref = refs.pop(0) if last else None
+    if not last:
+        totals, mass = refs.pop(0), refs.pop(0)
+    images, weights, moved, meta_vmem, meta, active, image_sem, meta_sem = refs[:8]
+    if last:
+        totals, mass = refs[8:10]
+    given_sem = refs[-1]
     depth, wave = images.shape[0], images.shape[1]
-    size = image_refs[0].shape[0]
-    per_row = weight_refs[0].shape[0]
+    per_row = weight_rows
+    chunk = weight_refs[0].shape[0]
     classes = lines // 2
-    waves = count * size // wave
+    waves = sum(ref.shape[0] for ref in image_refs) // wave
 
     def copies(w):
-        if size <= wave:
-            each = wave // size
-            return [
-                pltpu.make_async_copy(
-                    image_refs[w * each + b], images.at[w % depth, pl.ds(b * size, size)], image_sem.at[w % depth, b]
-                )
-                for b in range(each)
-            ]
-        return [
-            pltpu.make_async_copy(
-                image_refs[0].at[pl.ds(w * wave, wave)], images.at[w % depth], image_sem.at[w % depth, 0]
-            )
-        ]
+        out, at = [], 0
+        for b, ref in enumerate(image_refs):
+            size = ref.shape[0]
+            low, high = max(at, w * wave), min(at + size, (w + 1) * wave)
+            if low < high:
+                source = ref.at[pl.ds(low - at, high - low)]
+                target = images.at[w % depth, pl.ds(low - w * wave, high - low)]
+                out.append(pltpu.make_async_copy(source, target, image_sem.at[w % depth, b]))
+            at += size
+        return out
 
     for w in range(min(depth, waves)):
         for copy in copies(w):
             copy.start()
+    if first:
+        mass[...] = jnp.zeros_like(mass)
+        totals[...] = jnp.zeros_like(totals)
+    else:
+        held = [pltpu.make_async_copy(g, t, given_sem.at[k]) for k, (g, t) in enumerate(zip(given, (totals, mass)))]
+        for copy in held:
+            copy.start()
     moved[...] = jnp.zeros_like(moved)
-    mass[...] = jnp.zeros_like(mass)
-    totals[...] = jnp.zeros_like(totals)
     for b in range(n_weights):
-        weights[b * per_row : (b + 1) * per_row, :] = weight_refs[b][...].astype(jnp.float32)
+        weights[b * chunk : (b + 1) * chunk, :] = weight_refs[b][...].astype(jnp.float32)
     my_cls, my_dom = place_ref[0], place_ref[1]
     my_z, my_y = lax.div(my_dom, y_size), lax.rem(my_dom, y_size)
     lane = lax.broadcasted_iota(jnp.int32, (lines, LANES), 1)
@@ -376,6 +383,9 @@
             read_meta(here[i, IMAGE_ROWS:, :], meta_vmem, i)
         move_metas(meta_vmem, meta, meta_sem)
         number = collect(meta, active, wave, my_cls)
+        if w == 0 and not first:
+            for copy in held:
+                copy.wait()
 
         def prepare_one(i, share, buffer):
             side = side_of(meta, i, my_cls)
@@ -383,7 +393,7 @@
             if relative:
                 d_z = lax.rem(my_z - lax.div(q, y_size) + z_size, z_size)
                 d_y = lax.rem(my_y - lax.rem(q, y_size) + y_size, y_size)
-                q = d_y * z_size + d_z
+                q = d_z * y_size + d_y
             at = pl.multiple_of(q * per_row + meta[i, SLOT + side] * lines, lines)
             mine = weights[pl.ds(at, lines), :] * share
             values = here[i, :IMAGE_ROWS, :].astype(jnp.float32)
@@ -444,6 +454,8 @@
             for copy in copies(w + depth):
                 copy.start()
 
+    if not last:
+        return
     scale = 1.0 / (jnp.sum(mass[:local, :], axis=1, keepdims=True) + PRIOR_MASS)
     for turn in range(ROT):
         for tile in range(width // LANES):
@@ -451,32 +463,44 @@
             out_ref[:, pl.ds(turn * width + tile * LANES, LANES)] = (line * scale).astype(out_ref.dtype)
 
 
-def class_sum(place, buffers, weights, tables, relative, z_size, y_size, local, width, lines):
-    count, size = len(buffers), buffers[0].shape[0]
-    total = count * size
-    wave = math.gcd(total, 128)
+def class_sum(place, buffers, weights, tables, given, last, relative, z_size, y_size, local, width, lines, weight_rows):
+    count = len(buffers)
+    total = sum(buffer.shape[0] for buffer in buffers)
+    wave = total if total <= 128 else math.gcd(total, 128)
     depth = min(2, total // wave)
+    totals = (width // LANES * local * SPAN, LANES)
+    mass = (-(-local // 8) * 8, LANES)
+    first = given is None
+    out = jax.ShapeDtypeStruct((local, ROT * width), jnp.bfloat16)
+    held = tuple(jax.ShapeDtypeStruct(shape, jnp.float32) for shape in (totals, mass))
+    scratch = [
+        pltpu.VMEM((depth, wave, IMAGE_ROWS + META_ROWS, LANES), jnp.bfloat16),
+        pltpu.VMEM((len(weights) * weights[0].shape[0], LANES), jnp.float32),
+        pltpu.VMEM((2, 2 * LANES, width), jnp.bfloat16),
+        pltpu.VMEM((wave, LANES), jnp.int32),
+        pltpu.SMEM((wave, LANES), jnp.int32),
+        pltpu.SMEM((wave + 1,), jnp.int32),
+        pltpu.SemaphoreType.DMA((depth, count)),
+        pltpu.SemaphoreType.DMA,
+    ]
+    if last:
+        scratch += [pltpu.VMEM(totals, jnp.float32), pltpu.VMEM(mass, jnp.float32)]
+    scratch += [pltpu.SemaphoreType.DMA((2,))]
     return pl.pallas_call(
-        functools.partial(sum_kernel, relative, z_size, y_size, lines, count, len(weights)),
-        out_shape=jax.ShapeDtypeStruct((local, ROT * width), jnp.bfloat16),
-        in_specs=[SMEM_SPEC] + [HBM_SPEC] * count + [VMEM_SPEC] * (len(weights) + 1),
-        out_specs=VMEM_SPEC,
-        scratch_shapes=[
-            pltpu.VMEM((depth, wave, IMAGE_ROWS + META_ROWS, LANES), jnp.bfloat16),
-            pltpu.VMEM((len(weights) * weights[0].shape[0], LANES), jnp.float32),
-            pltpu.VMEM((2, 2 * LANES, width), jnp.bfloat16),
-            pltpu.VMEM((width // LANES * local * SPAN, LANES), jnp.float32),
-            pltpu.VMEM((-(-local // 8) * 8, LANES), jnp.float32),
-            pltpu.VMEM((wave, LANES), jnp.int32),
-            pltpu.SMEM((wave, LANES), jnp.int32),
-            pltpu.SMEM((wave + 1,), jnp.int32),
-            pltpu.SemaphoreType.DMA((depth, max(1, wave // size))),
-            pltpu.SemaphoreType.DMA,
-        ],
+        functools.partial(
+            sum_kernel, weight_rows, relative, z_size, y_size, lines, local, width, count, len(weights), first, last
+        ),
+        out_shape=out if last else held,
+        in_specs=[SMEM_SPEC]
+        + [HBM_SPEC] * count
+        + [VMEM_SPEC] * (len(weights) + 1)
+        + ([] if first else [HBM_SPEC] * 2),
+        out_specs=VMEM_SPEC if last else (VMEM_SPEC, VMEM_SPEC),
+        scratch_shapes=scratch,
         compiler_params=pltpu.CompilerParams(vmem_limit_bytes=VMEM_LIMIT),
-        cost_estimate=pl.CostEstimate(flops=2 * 10**10, bytes_accessed=10**7, transcendentals=0),
+        cost_estimate=pl.CostEstimate(flops=total * 2 * 10**8, bytes_accessed=10**7, transcendentals=0),
         name="class_sum",
-    )(place, *buffers, *weights, tables)
+    )(place, *buffers, *weights, tables, *([] if first else given))
 
 
 def shards(x_size, y_size, z_size, particles, references, candidates, offsets):
@@ -487,7 +511,7 @@
     classes = candidates.shape[1] // 2
     block_width = width // ROT
     slots = groups * (count // 2)
-    tables = jnp.asarray(trig_tables())
+    tables = trig_tables()
     place = jnp.stack([lax.axis_index("cls"), lax.axis_index("dom")]).astype(jnp.int32)
 
     def moves(goal):
@@ -504,29 +528,27 @@
 
     swap = functools.partial(send, goal=lambda x, c, z, y: (x, 1 - c, z, y))
     along_z = functools.partial(send, goal=lambda x, c, z, y: (x, c, z + 1, y))
+    back_z = functools.partial(send, goal=lambda x, c, z, y: (x, c, z - 1, y))
     early = functools.partial(send, goal=lambda x, c, z, y: (x + 1 - c, c, z, y + c))
     late = functools.partial(send, goal=lambda x, c, z, y: (x + c, c, z, y + 1 - c))
 
     images = particles.reshape(count, width // LANES, LANES)
     record = jnp.concatenate([candidates, offsets], axis=1)
-    mine, rest = prepare(place, record, swap(record), images, swap(images), tables, local)
+    mine, rest = prepare(place, record, swap(record), images, swap(images), jnp.asarray(tables), local)
     refs = references.reshape(local, ROT, block_width)
-    tuned = x_size == 2 and y_size == 2
+    steps = jnp.asarray(tables[:, 1])
+    tuned = x_size == 2 and y_size == 2 and z_size == 4
     if tuned:
-        first_early, first_late = early(mine), late(mine)
-        row = [mine, rest, first_early, first_late, swap(first_early), swap(first_late)]
-        ring = [mine]
-        for _ in range(z_size - 1):
-            ring.append(along_z(ring[-1]))
-        second = [first_early] + [early(part) for part in ring[1:]]
-        third = [first_late] + [late(part) for part in ring[1:] + second]
-        received = ring[1:] + second[1:] + third[1:]
-        buffers = row + received + [swap(part) for part in received]
+        e0, l0, z1 = early(mine), late(mine), along_z(mine)
+        e0, l0, z1, refs = lax.optimization_barrier((e0, l0, z1, refs))
+        row = [mine, rest, e0, l0, swap(e0), swap(l0)]
+        e1, l1, z2, f0 = early(z1), late(z1), along_z(z1), late(e0)
+        z3 = back_z(lax.optimization_barrier((mine, z1))[0])
     else:
         row = [lax.all_gather(mine, "cls", axis=0, tiled=True)]
-        buffers = [lax.all_gather(row[0], "dom", axis=0, tiled=True)]
-
-    weights, stats, partners = score(place, row, refs, tables, slots, classes)
+        parts = [[lax.all_gather(row[0], "dom", axis=0, tiled=True)]]
+
+    weights, stats, partners = score(place, row, refs, steps, slots, classes, [z1] if tuned else [])
     if tuned:
         stats = [
             stats,
@@ -534,20 +556,29 @@
             send(stats, lambda x, c, z, y: (x + 1, c, z, y)),
             send(stats, lambda x, c, z, y: (x + 1, 1 - c, z, y)),
         ]
+        weights, z2, z3, e1, l1, f0 = lax.optimization_barrier((weights, z2, z3, e1, l1, f0))
+        z23 = jnp.concatenate([z2, z3])
+        e23, f1 = early(z23), late(e1)
+        weights = normalise(tuned, place, partners, weights, stats)
+        pair = jnp.concatenate([weights, send(weights, lambda x, c, z, y: (x, c, z, y + 1))])
+        pair, e23, f1, z23 = lax.optimization_barrier((pair, e23, f1, z23))
+        weights = [pair] + [send(pair, lambda x, c, z, y, dz=dz: (x, c, z + dz, y)) for dz in range(1, z_size)]
+        l23, f23 = late(z23), late(e23)
+        middle = [z1, e1, l1, f0, f1, e23]
+        parts = [row + middle + [z23] + [swap(block) for block in [z1, z2, z3, *middle[1:]]], [l23, f23]]
     else:
         stats = [lax.all_gather(stats, "cls", axis=0, tiled=False)]
-    weights = normalise(tuned, place, partners, weights, stats)
-    if tuned:
-        weights = [
-            weights if dz == dy == 0 else send(weights, lambda x, c, z, y, dz=dz, dy=dy: (x, c, z + dz, y + dy))
-            for dy in range(y_size)
-            for dz in range(z_size)
-        ]
-    else:
+        weights = normalise(tuned, place, partners, weights, stats)
         weights = [lax.all_gather(weights, "dom", axis=0, tiled=True)]
-    return class_sum(
-        place, buffers, weights, tables, tuned, z_size, y_size, local, block_width, 2 * classes
-    )
+    held = None
+    for k, part in enumerate(parts):
+        if k:
+            *part, _ = lax.optimization_barrier((*part, held[1]))
+            part = part + [swap(block) for block in part]
+        held = class_sum(
+            place, part, weights, steps, held, k == len(parts) - 1, tuned, z_size, y_size, local, block_width, 2 * classes, slots * 2 * classes
+        )
+    return held
 
 
 def solution(mesh):

time: 132 us -> 124 us (0.939)
  starting transfers between devices: 36.9 us -> 26.6 us
  Pallas kernels: 48.8 us -> 56 us
  waiting for transfers between devices: 31.4 us -> 25.2 us
    ppermute x42 -> x33, starting transfers between devices: 36.9 us -> 26.6 us  [send(): return lax.ppermute(value, ('cls', 'dom'), moves(goal))]
    pallas_call x2 -> x3, Pallas kernels: 43.1 us -> 50.3 us  [the longest x2 39.5 us: class_sum(): pl.pallas_call(functools.partial(sum_kernel, weight_rows, relative, z_siz...]
    ppermute x42 -> x33, waiting for transfers between devices: 31.4 us -> 25.2 us  [send(): return lax.ppermute(value, ('cls', 'dom'), moves(goal))]
    unnamed x88 -> x71, local copies, waits for them, and re-layouts: 5.63 us -> 6.16 us
  transfers between devices with their start and end apart: 42 -> 33, of which waited for: 11 -> 11; matrix products, arithmetic and copies ran while one was open for 7% -> 8% of each run, Pallas kernels for 10% -> 30%
where the time goes in v3:
time: 124 us
  Pallas kernels  56 us (45%)
  starting transfers between devices  26.6 us (21%)
  waiting for transfers between devices  25.2 us (20%)
  local copies, waits for them, and re-layouts  13.3 us (11%)
  other arithmetic  2.13 us (2%)
    pallas_call x2, Pallas kernels, class_sum(): pl.pallas_call(functools.partial(sum_kernel, weight_rows, relative, z_siz...  39.5 us
    ppermute x33, starting transfers between devices, send(): return lax.ppermute(value, ('cls', 'dom'), moves(goal))  26.6 us
    ppermute x33, waiting for transfers between devices, send(): return lax.ppermute(value, ('cls', 'dom'), moves(goal))  25.2 us
    pallas_call x1, Pallas kernels, score(): pl.pallas_call(functools.partial(score_kernel, count, len(after)), out_sh...  10.9 us
    reshape x1, local copies, waits for them, and re-layouts, shards(): refs = references.reshape(local, ROT, block_width)  7.11 us
    unnamed x71, local copies, waits for them, and re-layouts  6.16 us
    pallas_call x1, Pallas kernels, prepare(): pl.pallas_call(functools.partial(prep_kernel, local), out_shape=(shape, s...  4.09 us
  transfers between devices with their start and end apart: 33, of which 11 were waited for; matrix products, arithmetic and copies ran while one was open for 8% of the time, Pallas kernels for 30%

profile of v3, /device:TPU:0, one launch (start us, length us, event | category | flops | bytes accessed | tf_op | source)
XLA Modules:
  0.0 123.6 jit_solution(16298217134002784038)
XLA Ops:
  0.0 1.0 copy.10
  1.5 0.8 copy.7
  2.3 0.8 pad_add_fusion.near_ref
  5.5 4.1 %prepare.1 = (bf16[4,336,128]{2,1,0:T(8,128)(2,1)}, bf16[4,336,128]{2,1,0:T(8,128)(2,1)}) custom-call(s32[2]{0:T(128)} %pad_add_fusion.1.place_ref, s32[4,10]{1,0:T(4,128)} %copy-done.7, s32[4,10]{1,0:T(4,128)} %copy-done.8, bf16[4,288,128]{2,1,0:T(8,128)(2,1)} %bitcast.7, bf16[4,288,128]{2,1,0:T(8,128)(2,1)} %copy-done.1, ...), custom_call_target="tpu_custom_call" | custom-call | tf_op jit(solution)/shard_map/prepare/pallas_call | solution.py:133
  9.6 2.7 %collective-permute-start.2 = (bf16[4,336,128]{2,1,0:T(8,128)(2,1)}, bf16[4,336,128]{2,1,0:T(8,128)(2,1)S(1)}, u32[]{:S(2)}, u32[]{:S(2)}) collective-permute-start(bf16[4,336,128]{2,1,0:T(8,128)(2,1)} %get-tuple-element.37.refs_0_), channel_id=1, source_target_pairs={{0,16},{1,17},{2,18},{3,19},{4,20},{5,21},{6,22},{7,23},{8,9},{9,8... | collective-permute-start | bytes 1032200 | tf_op jit(solution)/shard_map/ppermute | solution.py:527
  12.3 1.5 %collective-permute-start.3 = (bf16[4,336,128]{2,1,0:T(8,128)(2,1)}, bf16[4,336,128]{2,1,0:T(8,128)(2,1)S(1)}, u32[]{:S(2)}, u32[]{:S(2)}) collective-permute-start(bf16[4,336,128]{2,1,0:T(8,128)(2,1)} %get-tuple-element.37.refs_0_), channel_id=1, source_target_pairs={{0,1},{1,0},{2,3},{3,2},{4,5},{5,4},{6,7},{7,6},{8,24},{9,25},{10,... | collective-permute-start | bytes 1032200 | tf_op jit(solution)/shard_map/ppermute | solution.py:527
  13.8 1.6 %collective-permute-start.4 = (bf16[4,336,128]{2,1,0:T(8,128)(2,1)}, bf16[4,336,128]{2,1,0:T(8,128)(2,1)S(1)}, u32[]{:S(2)}, u32[]{:S(2)}) collective-permute-start(bf16[4,336,128]{2,1,0:T(8,128)(2,1)} %get-tuple-element.37.refs_0_), channel_id=1, source_target_pairs={{0,2},{1,3},{2,4},{3,5},{4,6},{5,7},{6,0},{7,1},{8,10},{9,11},{10,... | collective-permute-start | bytes 1032200 | tf_op jit(solution)/shard_map/ppermute | solution.py:527
  15.4 7.1 %reshape.7.refs_7_ = bf16[50,36,1024]{2,1,0:T(8,128)(2,1)} reshape(bf16[50,36864]{1,0:T(8,128)(2,1)} %param.7) | data formatting | bytes 7372800 | tf_op jit(solution)/shard_map/reshape | solution.py:538
  22.5 3.1 %collective-permute-done.4.refs_6_ = bf16[4,336,128]{2,1,0:T(8,128)(2,1)S(1)} collective-permute-done((bf16[4,336,128]{2,1,0:T(8,128)(2,1)}, bf16[4,336,128]{2,1,0:T(8,128)(2,1)S(1)}, u32[]{:S(2)}, u32[]{:S(2)}) %collective-permute-start.4) | collective-permute-done | bytes 344096 | tf_op jit(solution)/shard_map/ppermute | solution.py:527
  27.3 1.4 %collective-permute-start.11 = (bf16[4,336,128]{2,1,0:T(8,128)(2,1)S(1)}, bf16[4,336,128]{2,1,0:T(8,128)(2,1)S(1)}, u32[]{:S(2)}, u32[]{:S(2)}) collective-permute-start(bf16[4,336,128]{2,1,0:T(8,128)(2,1)S(1)} %collective-permute-done.2.refs_2_), channel_id=1, source_target_pairs={{0,1},{1,0},{2,3},{3,2},{4,5},{5,4},{6,7},{7,6},{8,24},{9,25},{10,... | collective-permute-start | bytes 1032200 | tf_op jit(solution)/shard_map/ppermute | solution.py:527
  28.7 3.9 %collective-permute-start.8 = (bf16[4,336,128]{2,1,0:T(8,128)(2,1)S(1)}, bf16[4,336,128]{2,1,0:T(8,128)(2,1)S(1)}, u32[]{:S(2)}, u32[]{:S(2)}) collective-permute-start(bf16[4,336,128]{2,1,0:T(8,128)(2,1)S(1)} %copy-done.15), channel_id=1, source_target_pairs={{0,6},{1,7},{2,0},{3,1},{4,2},{5,3},{6,4},{7,5},{8,14},{9,15},{10,... | collective-permute-start | bytes 1032200 | tf_op jit(solution)/shard_map/ppermute | solution.py:527
  32.6 10.9 %score.1 = (f32[8,8,128]{2,1,0:T(8,128)}, f32[16,128]{1,0:T(8,128)}, s32[8,3]{1,0:T(8,128)}) custom-call(s32[2]{0:T(128)} %pad_add_fusion.1.place_ref, bf16[4,336,128]{2,1,0:T(8,128)(2,1)} %get-tuple-element.37.refs_0_, bf16[4,336,128]{2,1,0:T(8,128)(2,1)} %get-tuple-element.30.refs_1_, bf16[4,336,128]{2,1,0:T(8,128)(2,1)} %copy-done.16, ...), custom_call_target="tpu_custom_call" | custom-call | flops 10000000000 | bytes 10000000 | tf_op jit(solution)/shard_map/score/pallas_call | solution.py:271
  43.5 1.8 %collective-permute-done.8 = bf16[4,336,128]{2,1,0:T(8,128)(2,1)S(1)} collective-permute-done((bf16[4,336,128]{2,1,0:T(8,128)(2,1)S(1)}, bf16[4,336,128]{2,1,0:T(8,128)(2,1)S(1)}, u32[]{:S(2)}, u32[]{:S(2)}) %collective-permute-start.8) | collective-permute-done | bytes 344096 | tf_op jit(solution)/shard_map/ppermute | solution.py:527
  45.4 1.4 %collective-permute-start.16 = (bf16[8,336,128]{2,1,0:T(8,128)(2,1)S(1)}, bf16[8,336,128]{2,1,0:T(8,128)(2,1)S(1)}, u32[]{:S(2)}, u32[]{:S(2)}) collective-permute-start(bf16[8,336,128]{2,1,0:T(8,128)(2,1)S(1)} %constant_dynamic-update-slice_fusion.refs_12_), channel_id=1, source_target_pairs={{0,16},{1,17},{2,18},{3,19},{4,20},{5,21},{6,22},{7,23},{8,9},{9,8... | collective-permute-start | bytes 2064392 | tf_op jit(solution)/shard_map/ppermute | solution.py:527
  46.8 0.7 collective-permute-start.17
  47.5 0.8 collective-permute-start.13
  48.3 1.1 collective-permute-start.14
  49.4 10.5 %collective-permute-done.13.refs_2_ = f32[16,128]{1,0:T(8,128)S(1)} collective-permute-done((f32[16,128]{1,0:T(8,128)}, f32[16,128]{1,0:T(8,128)S(1)}, u32[]{:S(2)}, u32[]{:S(2)}) %collective-permute-start.13) | collective-permute-done | bytes 8224 | tf_op jit(solution)/shard_map/ppermute | solution.py:527
  60.5 1.5 %normalise.1 = bf16[64,128]{1,0:T(8,128)(2,1)} custom-call(s32[2]{0:T(128)} %pad_add_fusion.1.place_ref, s32[8,3]{1,0:T(8,128)} %get-tuple-element.35.partner_ref, f32[8,8,128]{2,1,0:T(8,128)} %get-tuple-element.38.weight_ref, f32[16,128]{1,0:T(8,128)} %get-tuple-element.39.refs_0_, f32[16,128]{1,0:T(8,128)} %copy-done.4, f32[16,128]{1,0:T(8,128)} %copy-done.5, ...), custom_call_target="tpu_custom_call" | custom-call | tf_op jit(solution)/shard_map/normalise/pallas_call | solution.py:320
  62.1 0.8 collective-permute-start.15
  63.4 2.6 %collective-permute-done.15 = bf16[64,128]{1,0:T(8,128)(2,1)S(1)} collective-permute-done((bf16[64,128]{1,0:T(8,128)(2,1)}, bf16[64,128]{1,0:T(8,128)(2,1)S(1)}, u32[]{:S(2)}, u32[]{:S(2)}) %collective-permute-start.15) | collective-permute-done | bytes 16416 | tf_op jit(solution)/shard_map/ppermute | solution.py:527
  68.4 1.8 %collective-permute-done.23.refs_16_ = bf16[4,336,128]{2,1,0:T(8,128)(2,1)S(1)} collective-permute-done((bf16[4,336,128]{2,1,0:T(8,128)(2,1)}, bf16[4,336,128]{2,1,0:T(8,128)(2,1)S(1)}, u32[]{:S(2)}, u32[]{:S(2)}) %collective-permute-start.23) | collective-permute-done | bytes 344096 | tf_op jit(solution)/shard_map/ppermute | solution.py:527
  70.8 3.3 %collective-permute-start.30 = (bf16[128,128]{1,0:T(8,128)(2,1)S(1)}, bf16[128,128]{1,0:T(8,128)(2,1)S(1)}, u32[]{:S(2)}, u32[]{:S(2)}) collective-permute-start(bf16[128,128]{1,0:T(8,128)(2,1)S(1)} %pad_maximum_fusion.refs_21_.refs_4_), channel_id=1, source_target_pairs={{0,6},{1,7},{2,0},{3,1},{4,2},{5,3},{6,4},{7,5},{8,14},{9,15},{10,... | collective-permute-start | bytes 98312 | tf_op jit(solution)/shard_map/ppermute | solution.py:527
  74.1 2.1 %collective-permute-done.28.refs_22_.refs_5_ = bf16[128,128]{1,0:T(8,128)(2,1)S(1)} collective-permute-done((bf16[128,128]{1,0:T(8,128)(2,1)S(1)}, bf16[128,128]{1,0:T(8,128)(2,1)S(1)}, u32[]{:S(2)}, u32[]{:S(2)}) %collective-permute-start.28) | collective-permute-done | bytes 32800 | tf_op jit(solution)/shard_map/ppermute | solution.py:527
  76.9 1.4 %collective-permute-start.18 = (bf16[8,336,128]{2,1,0:T(8,128)(2,1)S(1)}, bf16[8,336,128]{2,1,0:T(8,128)(2,1)S(1)}, u32[]{:S(2)}, u32[]{:S(2)}) collective-permute-start(bf16[8,336,128]{2,1,0:T(8,128)(2,1)S(1)} %constant_dynamic-update-slice_fusion.refs_12_), channel_id=1, source_target_pairs={{0,1},{1,0},{2,3},{3,2},{4,5},{5,4},{6,7},{7,6},{8,24},{9,25},{10,... | collective-permute-start | bytes 2064392 | tf_op jit(solution)/shard_map/ppermute | solution.py:527
  78.4 0.7 copy-done.30
  79.2 0.8 copy-done.10
  80.0 24.7 %class_sum.2 = (f32[16000,128]{1,0:T(8,128)}, f32[56,128]{1,0:T(8,128)}) custom-call(s32[2]{0:T(128)} %pad_add_fusion.1.place_ref, bf16[4,336,128]{2,1,0:T(8,128)(2,1)} %get-tuple-element.37.refs_0_, bf16[4,336,128]{2,1,0:T(8,128)(2,1)} %get-tuple-element.30.refs_1_, bf16[4,336,128]{2,1,0:T(8,128)(2,1)} %copy-done.16, bf16[4,336,128]{2,1,0:T(8,128)(2,1)} %copy-done.17, ...), custom_call_target="tpu_custom_call" | custom-call | flops 19200000000 | bytes 10000000 | tf_op jit(solution)/shard_map/class_sum/pallas_call | solution.py:489
  105.4 1.6 %collective-permute-done.31.refs_2_ = bf16[8,336,128]{2,1,0:T(8,128)(2,1)S(1)} collective-permute-done((bf16[8,336,128]{2,1,0:T(8,128)(2,1)S(1)}, bf16[8,336,128]{2,1,0:T(8,128)(2,1)S(1)}, u32[]{:S(2)}, u32[]{:S(2)}) %collective-permute-start.31) | collective-permute-done | bytes 688160 | tf_op jit(solution)/shard_map/ppermute | solution.py:527
  107.0 1.0 collective-permute-done.32.refs_3_
  108.0 0.8 copy-done.14
  108.8 14.7 %class_sum.3 = bf16[50,36864]{1,0:T(8,128)(2,1)} custom-call(s32[2]{0:T(128)} %pad_add_fusion.1.place_ref, bf16[8,336,128]{2,1,0:T(8,128)(2,1)} %copy-done.12, bf16[8,336,128]{2,1,0:T(8,128)(2,1)} %copy-done.11, bf16[8,336,128]{2,1,0:T(8,128)(2,1)} %copy-done.13, bf16[8,336,128]{2,1,0:T(8,128)(2,1)} %copy-done.14, bf16[128,128]{1,0:T(8,128)(2,1)} %copy-done.3, ...), custom_call_target="tpu_custom_call" | custom-call | flops 6400000000 | bytes 10000000 | tf_op jit(solution)/shard_map/class_sum/pallas_call | solution.py:489
  (115 shorter events, 10.1 us)
Async XLA Ops:
  1.0 3.2 %collective-permute-start.1 = (bf16[4,288,128]{2,1,0:T(8,128)(2,1)S(1)}, bf16[4,288,128]{2,1,0:T(8,128)(2,1)S(1)}, u32[]{:S(2)}, u32[]{:S(2)}) collective-permute-start(bf16[4,288,128]{2,1,0:T(8,128)(2,1)S(1)} %bitcast.6), channel_id=1, source_target_pairs={{0,8},{1,9},{2,10},{3,11},{4,12},{5,13},{6,14},{7,15},{8,0},{9,1},... | collective-permute-start | bytes 884744 | tf_op jit(solution)/shard_map/ppermute | solution.py:527
  9.6 12.9 %collective-permute-start.2 = (bf16[4,336,128]{2,1,0:T(8,128)(2,1)}, bf16[4,336,128]{2,1,0:T(8,128)(2,1)S(1)}, u32[]{:S(2)}, u32[]{:S(2)}) collective-permute-start(bf16[4,336,128]{2,1,0:T(8,128)(2,1)} %get-tuple-element.37.refs_0_), channel_id=1, source_target_pairs={{0,16},{1,17},{2,18},{3,19},{4,20},{5,21},{6,22},{7,23},{8,9},{9,8... | collective-permute-start | bytes 1032200 | tf_op jit(solution)/shard_map/ppermute | solution.py:527
  12.3 10.2 %collective-permute-start.3 = (bf16[4,336,128]{2,1,0:T(8,128)(2,1)}, bf16[4,336,128]{2,1,0:T(8,128)(2,1)S(1)}, u32[]{:S(2)}, u32[]{:S(2)}) collective-permute-start(bf16[4,336,128]{2,1,0:T(8,128)(2,1)} %get-tuple-element.37.refs_0_), channel_id=1, source_target_pairs={{0,1},{1,0},{2,3},{3,2},{4,5},{5,4},{6,7},{7,6},{8,24},{9,25},{10,... | collective-permute-start | bytes 1032200 | tf_op jit(solution)/shard_map/ppermute | solution.py:527
  13.8 11.8 %collective-permute-start.4 = (bf16[4,336,128]{2,1,0:T(8,128)(2,1)}, bf16[4,336,128]{2,1,0:T(8,128)(2,1)S(1)}, u32[]{:S(2)}, u32[]{:S(2)}) collective-permute-start(bf16[4,336,128]{2,1,0:T(8,128)(2,1)} %get-tuple-element.37.refs_0_), channel_id=1, source_target_pairs={{0,2},{1,3},{2,4},{3,5},{4,6},{5,7},{6,0},{7,1},{8,10},{9,11},{10,... | collective-permute-start | bytes 1032200 | tf_op jit(solution)/shard_map/ppermute | solution.py:527
  25.6 1.7 %collective-permute-start.5 = (bf16[4,336,128]{2,1,0:T(8,128)(2,1)S(1)}, bf16[4,336,128]{2,1,0:T(8,128)(2,1)S(1)}, u32[]{:S(2)}, u32[]{:S(2)}) collective-permute-start(bf16[4,336,128]{2,1,0:T(8,128)(2,1)S(1)} %collective-permute-done.2.refs_2_), channel_id=1, source_target_pairs={{0,8},{1,9},{2,10},{3,11},{4,12},{5,13},{6,14},{7,15},{8,0},{9,1},... | collective-permute-start | bytes 1032200 | tf_op jit(solution)/shard_map/ppermute | solution.py:527
  25.6 3.1 %collective-permute-start.6 = (bf16[4,336,128]{2,1,0:T(8,128)(2,1)S(1)}, bf16[4,336,128]{2,1,0:T(8,128)(2,1)S(1)}, u32[]{:S(2)}, u32[]{:S(2)}) collective-permute-start(bf16[4,336,128]{2,1,0:T(8,128)(2,1)S(1)} %collective-permute-done.3.refs_3_), channel_id=1, source_target_pairs={{0,8},{1,9},{2,10},{3,11},{4,12},{5,13},{6,14},{7,15},{8,0},{9,1},... | collective-permute-start | bytes 1032200 | tf_op jit(solution)/shard_map/ppermute | solution.py:527
  26.1 19.1 %collective-permute-start.10 = (bf16[4,336,128]{2,1,0:T(8,128)(2,1)S(1)}, bf16[4,336,128]{2,1,0:T(8,128)(2,1)S(1)}, u32[]{:S(2)}, u32[]{:S(2)}) collective-permute-start(bf16[4,336,128]{2,1,0:T(8,128)(2,1)S(1)} %collective-permute-done.4.refs_6_), channel_id=1, source_target_pairs={{0,1},{1,0},{2,3},{3,2},{4,5},{5,4},{6,7},{7,6},{8,24},{9,25},{10,... | collective-permute-start | bytes 1032200 | tf_op jit(solution)/shard_map/ppermute | solution.py:527
  26.6 18.6 %collective-permute-start.7 = (bf16[4,336,128]{2,1,0:T(8,128)(2,1)S(1)}, bf16[4,336,128]{2,1,0:T(8,128)(2,1)S(1)}, u32[]{:S(2)}, u32[]{:S(2)}) collective-permute-start(bf16[4,336,128]{2,1,0:T(8,128)(2,1)S(1)} %collective-permute-done.4.refs_6_), channel_id=1, source_target_pairs={{0,2},{1,3},{2,4},{3,5},{4,6},{5,7},{6,0},{7,1},{8,10},{9,11},{10,... | collective-permute-start | bytes 1032200 | tf_op jit(solution)/shard_map/ppermute | solution.py:527
  26.6 18.6 %collective-permute-start.9 = (bf16[4,336,128]{2,1,0:T(8,128)(2,1)S(1)}, bf16[4,336,128]{2,1,0:T(8,128)(2,1)S(1)}, u32[]{:S(2)}, u32[]{:S(2)}) collective-permute-start(bf16[4,336,128]{2,1,0:T(8,128)(2,1)S(1)} %collective-permute-done.4.refs_6_), channel_id=1, source_target_pairs={{0,16},{1,17},{2,18},{3,19},{4,20},{5,21},{6,22},{7,23},{8,9},{9,8... | collective-permute-start | bytes 1032200 | tf_op jit(solution)/shard_map/ppermute | solution.py:527
  27.3 18.0 %collective-permute-start.11 = (bf16[4,336,128]{2,1,0:T(8,128)(2,1)S(1)}, bf16[4,336,128]{2,1,0:T(8,128)(2,1)S(1)}, u32[]{:S(2)}, u32[]{:S(2)}) collective-permute-start(bf16[4,336,128]{2,1,0:T(8,128)(2,1)S(1)} %collective-permute-done.2.refs_2_), channel_id=1, source_target_pairs={{0,1},{1,0},{2,3},{3,2},{4,5},{5,4},{6,7},{7,6},{8,24},{9,25},{10,... | collective-permute-start | bytes 1032200 | tf_op jit(solution)/shard_map/ppermute | solution.py:527
  28.7 16.5 %collective-permute-start.8 = (bf16[4,336,128]{2,1,0:T(8,128)(2,1)S(1)}, bf16[4,336,128]{2,1,0:T(8,128)(2,1)S(1)}, u32[]{:S(2)}, u32[]{:S(2)}) collective-permute-start(bf16[4,336,128]{2,1,0:T(8,128)(2,1)S(1)} %copy-done.15), channel_id=1, source_target_pairs={{0,6},{1,7},{2,0},{3,1},{4,2},{5,3},{6,4},{7,5},{8,14},{9,15},{10,... | collective-permute-start | bytes 1032200 | tf_op jit(solution)/shard_map/ppermute | solution.py:527
  45.4 21.4 %collective-permute-start.16 = (bf16[8,336,128]{2,1,0:T(8,128)(2,1)S(1)}, bf16[8,336,128]{2,1,0:T(8,128)(2,1)S(1)}, u32[]{:S(2)}, u32[]{:S(2)}) collective-permute-start(bf16[8,336,128]{2,1,0:T(8,128)(2,1)S(1)} %constant_dynamic-update-slice_fusion.refs_12_), channel_id=1, source_target_pairs={{0,16},{1,17},{2,18},{3,19},{4,20},{5,21},{6,22},{7,23},{8,9},{9,8... | collective-permute-start | bytes 2064392 | tf_op jit(solution)/shard_map/ppermute | solution.py:527
  46.8 20.0 %collective-permute-start.17 = (bf16[4,336,128]{2,1,0:T(8,128)(2,1)S(1)}, bf16[4,336,128]{2,1,0:T(8,128)(2,1)}, u32[]{:S(2)}, u32[]{:S(2)}) collective-permute-start(bf16[4,336,128]{2,1,0:T(8,128)(2,1)S(1)} %collective-permute-done.9.refs_7_), channel_id=1, source_target_pairs={{0,1},{1,0},{2,3},{3,2},{4,5},{5,4},{6,7},{7,6},{8,24},{9,25},{10,... | collective-permute-start | bytes 1032200 | tf_op jit(solution)/shard_map/ppermute | solution.py:527
  47.5 1.9 %collective-permute-start.12 = (f32[16,128]{1,0:T(8,128)}, f32[16,128]{1,0:T(8,128)S(1)}, u32[]{:S(2)}, u32[]{:S(2)}) collective-permute-start(f32[16,128]{1,0:T(8,128)} %get-tuple-element.39.refs_0_), channel_id=1, source_target_pairs={{0,8},{1,9},{2,10},{3,11},{4,12},{5,13},{6,14},{7,15},{8,0},{9,1},... | collective-permute-start | bytes 24584 | tf_op jit(solution)/shard_map/ppermute | solution.py:527
  47.5 12.4 %collective-permute-start.13 = (f32[16,128]{1,0:T(8,128)}, f32[16,128]{1,0:T(8,128)S(1)}, u32[]{:S(2)}, u32[]{:S(2)}) collective-permute-start(f32[16,128]{1,0:T(8,128)} %get-tuple-element.39.refs_0_), channel_id=1, source_target_pairs={{0,16},{1,17},{2,18},{3,19},{4,20},{5,21},{6,22},{7,23},{8,24},{9,... | collective-permute-start | bytes 24584 | tf_op jit(solution)/shard_map/ppermute | solution.py:527
  48.3 11.6 %collective-permute-start.14 = (f32[16,128]{1,0:T(8,128)}, f32[16,128]{1,0:T(8,128)S(1)}, u32[]{:S(2)}, u32[]{:S(2)}) collective-permute-start(f32[16,128]{1,0:T(8,128)} %get-tuple-element.39.refs_0_), channel_id=1, source_target_pairs={{0,24},{1,25},{2,26},{3,27},{4,28},{5,29},{6,30},{7,31},{8,16},{9,... | collective-permute-start | bytes 24584 | tf_op jit(solution)/shard_map/ppermute | solution.py:527
  62.1 3.9 %collective-permute-start.15 = (bf16[64,128]{1,0:T(8,128)(2,1)}, bf16[64,128]{1,0:T(8,128)(2,1)S(1)}, u32[]{:S(2)}, u32[]{:S(2)}) collective-permute-start(bf16[64,128]{1,0:T(8,128)(2,1)} %normalise.1), channel_id=1, source_target_pairs={{0,1},{1,0},{2,3},{3,2},{4,5},{5,4},{6,7},{7,6},{8,9},{9,8},{10,11... | collective-permute-start | bytes 49160 | tf_op jit(solution)/shard_map/ppermute | solution.py:527
  62.9 4.5 %collective-permute-start.20 = (bf16[4,336,128]{2,1,0:T(8,128)(2,1)}, bf16[4,336,128]{2,1,0:T(8,128)(2,1)S(1)}, u32[]{:S(2)}, u32[]{:S(2)}) collective-permute-start(bf16[4,336,128]{2,1,0:T(8,128)(2,1)} %copy-done.18), channel_id=1, source_target_pairs={{0,8},{1,9},{2,10},{3,11},{4,12},{5,13},{6,14},{7,15},{8,0},{9,1},... | collective-permute-start | bytes 1032200 | tf_op jit(solution)/shard_map/ppermute | solution.py:527
  62.9 5.0 %collective-permute-start.21 = (bf16[4,336,128]{2,1,0:T(8,128)(2,1)S(1)}, bf16[4,336,128]{2,1,0:T(8,128)(2,1)S(1)}, u32[]{:S(2)}, u32[]{:S(2)}) collective-permute-start(bf16[4,336,128]{2,1,0:T(8,128)(2,1)S(1)} %collective-permute-done.7), channel_id=1, source_target_pairs={{0,8},{1,9},{2,10},{3,11},{4,12},{5,13},{6,14},{7,15},{8,0},{9,1},... | collective-permute-start | bytes 1032200 | tf_op jit(solution)/shard_map/ppermute | solution.py:527
  66.0 1.9 %collective-permute-start.22 = (bf16[4,336,128]{2,1,0:T(8,128)(2,1)S(1)}, bf16[4,336,128]{2,1,0:T(8,128)(2,1)S(1)}, u32[]{:S(2)}, u32[]{:S(2)}) collective-permute-start(bf16[4,336,128]{2,1,0:T(8,128)(2,1)S(1)} %collective-permute-done.8), channel_id=1, source_target_pairs={{0,8},{1,9},{2,10},{3,11},{4,12},{5,13},{6,14},{7,15},{8,0},{9,1},... | collective-permute-start | bytes 1032200 | tf_op jit(solution)/shard_map/ppermute | solution.py:527
  66.8 12.3 %collective-permute-start.27 = (bf16[8,336,128]{2,1,0:T(8,128)(2,1)S(1)}, bf16[8,336,128]{2,1,0:T(8,128)(2,1)S(1)}, u32[]{:S(2)}, u32[]{:S(2)}) collective-permute-start(bf16[8,336,128]{2,1,0:T(8,128)(2,1)S(1)} %collective-permute-done.16.refs_11_), channel_id=1, source_target_pairs={{0,8},{1,9},{2,10},{3,11},{4,12},{5,13},{6,14},{7,15},{8,0},{9,1},... | collective-permute-start | bytes 2064392 | tf_op jit(solution)/shard_map/ppermute | solution.py:527
  67.4 2.8 %collective-permute-start.23 = (bf16[4,336,128]{2,1,0:T(8,128)(2,1)}, bf16[4,336,128]{2,1,0:T(8,128)(2,1)S(1)}, u32[]{:S(2)}, u32[]{:S(2)}) collective-permute-start(bf16[4,336,128]{2,1,0:T(8,128)(2,1)} %copy-done.22), channel_id=1, source_target_pairs={{0,8},{1,9},{2,10},{3,11},{4,12},{5,13},{6,14},{7,15},{8,0},{9,1},... | collective-permute-start | bytes 1032200 | tf_op jit(solution)/shard_map/ppermute | solution.py:527
  67.4 3.3 %collective-permute-start.24 = (bf16[4,336,128]{2,1,0:T(8,128)(2,1)S(1)}, bf16[4,336,128]{2,1,0:T(8,128)(2,1)S(1)}, u32[]{:S(2)}, u32[]{:S(2)}) collective-permute-start(bf16[4,336,128]{2,1,0:T(8,128)(2,1)S(1)} %collective-permute-done.10.refs_8_), channel_id=1, source_target_pairs={{0,8},{1,9},{2,10},{3,11},{4,12},{5,13},{6,14},{7,15},{8,0},{9,1},... | collective-permute-start | bytes 1032200 | tf_op jit(solution)/shard_map/ppermute | solution.py:527
  67.9 2.9 %collective-permute-start.25 = (bf16[4,336,128]{2,1,0:T(8,128)(2,1)}, bf16[4,336,128]{2,1,0:T(8,128)(2,1)S(1)}, u32[]{:S(2)}, u32[]{:S(2)}) collective-permute-start(bf16[4,336,128]{2,1,0:T(8,128)(2,1)} %copy-done.23), channel_id=1, source_target_pairs={{0,8},{1,9},{2,10},{3,11},{4,12},{5,13},{6,14},{7,15},{8,0},{9,1},... | collective-permute-start | bytes 1032200 | tf_op jit(solution)/shard_map/ppermute | solution.py:527
  68.0 10.4 %collective-permute-start.26 = (bf16[4,336,128]{2,1,0:T(8,128)(2,1)}, bf16[4,336,128]{2,1,0:T(8,128)(2,1)S(1)}, u32[]{:S(2)}, u32[]{:S(2)}) collective-permute-start(bf16[4,336,128]{2,1,0:T(8,128)(2,1)} %collective-permute-done.17.refs_10_), channel_id=1, source_target_pairs={{0,8},{1,9},{2,10},{3,11},{4,12},{5,13},{6,14},{7,15},{8,0},{9,1},... | collective-permute-start | bytes 1032200 | tf_op jit(solution)/shard_map/ppermute | solution.py:527
  70.2 6.0 %collective-permute-start.28 = (bf16[128,128]{1,0:T(8,128)(2,1)S(1)}, bf16[128,128]{1,0:T(8,128)(2,1)S(1)}, u32[]{:S(2)}, u32[]{:S(2)}) collective-permute-start(bf16[128,128]{1,0:T(8,128)(2,1)S(1)} %pad_maximum_fusion.refs_21_.refs_4_), channel_id=1, source_target_pairs={{0,2},{1,3},{2,4},{3,5},{4,6},{5,7},{6,0},{7,1},{8,10},{9,11},{10,... | collective-permute-start | bytes 98312 | tf_op jit(solution)/shard_map/ppermute | solution.py:527
  70.8 6.2 %collective-permute-start.29 = (bf16[128,128]{1,0:T(8,128)(2,1)S(1)}, bf16[128,128]{1,0:T(8,128)(2,1)S(1)}, u32[]{:S(2)}, u32[]{:S(2)}) collective-permute-start(bf16[128,128]{1,0:T(8,128)(2,1)S(1)} %pad_maximum_fusion.refs_21_.refs_4_), channel_id=1, source_target_pairs={{0,4},{1,5},{2,6},{3,7},{4,0},{5,1},{6,2},{7,3},{8,12},{9,13},{10,... | collective-permute-start | bytes 98312 | tf_op jit(solution)/shard_map/ppermute | solution.py:527
  70.8 7.5 %collective-permute-start.30 = (bf16[128,128]{1,0:T(8,128)(2,1)S(1)}, bf16[128,128]{1,0:T(8,128)(2,1)S(1)}, u32[]{:S(2)}, u32[]{:S(2)}) collective-permute-start(bf16[128,128]{1,0:T(8,128)(2,1)S(1)} %pad_maximum_fusion.refs_21_.refs_4_), channel_id=1, source_target_pairs={{0,6},{1,7},{2,0},{3,1},{4,2},{5,3},{6,4},{7,5},{8,14},{9,15},{10,... | collective-permute-start | bytes 98312 | tf_op jit(solution)/shard_map/ppermute | solution.py:527
  76.2 28.6 %collective-permute-start.19 = (bf16[8,336,128]{2,1,0:T(8,128)(2,1)S(1)}, bf16[8,336,128]{2,1,0:T(8,128)(2,1)S(1)}, u32[]{:S(2)}, u32[]{:S(2)}) collective-permute-start(bf16[8,336,128]{2,1,0:T(8,128)(2,1)S(1)} %collective-permute-done.16.refs_11_), channel_id=1, source_target_pairs={{0,1},{1,0},{2,3},{3,2},{4,5},{5,4},{6,7},{7,6},{8,24},{9,25},{10,... | collective-permute-start | bytes 2064392 | tf_op jit(solution)/shard_map/ppermute | solution.py:527
  76.9 27.8 %collective-permute-start.18 = (bf16[8,336,128]{2,1,0:T(8,128)(2,1)S(1)}, bf16[8,336,128]{2,1,0:T(8,128)(2,1)S(1)}, u32[]{:S(2)}, u32[]{:S(2)}) collective-permute-start(bf16[8,336,128]{2,1,0:T(8,128)(2,1)S(1)} %constant_dynamic-update-slice_fusion.refs_12_), channel_id=1, source_target_pairs={{0,1},{1,0},{2,3},{3,2},{4,5},{5,4},{6,7},{7,6},{8,24},{9,25},{10,... | collective-permute-start | bytes 2064392 | tf_op jit(solution)/shard_map/ppermute | solution.py:527
  104.8 2.2 %collective-permute-start.31 = (bf16[8,336,128]{2,1,0:T(8,128)(2,1)S(1)}, bf16[8,336,128]{2,1,0:T(8,128)(2,1)S(1)}, u32[]{:S(2)}, u32[]{:S(2)}) collective-permute-start(bf16[8,336,128]{2,1,0:T(8,128)(2,1)S(1)} %collective-permute-done.18.refs_0_), channel_id=1, source_target_pairs={{0,8},{1,9},{2,10},{3,11},{4,12},{5,13},{6,14},{7,15},{8,0},{9,1},... | collective-permute-start | bytes 2064392 | tf_op jit(solution)/shard_map/ppermute | solution.py:527
  104.9 3.1 %collective-permute-start.32 = (bf16[8,336,128]{2,1,0:T(8,128)(2,1)S(1)}, bf16[8,336,128]{2,1,0:T(8,128)(2,1)S(1)}, u32[]{:S(2)}, u32[]{:S(2)}) collective-permute-start(bf16[8,336,128]{2,1,0:T(8,128)(2,1)S(1)} %collective-permute-done.19.refs_1_), channel_id=1, source_target_pairs={{0,8},{1,9},{2,10},{3,11},{4,12},{5,13},{6,14},{7,15},{8,0},{9,1},... | collective-permute-start | bytes 2064392 | tf_op jit(solution)/shard_map/ppermute | solution.py:527
  (35 other events, 273.2 us)
